TPU v7x, 32 devices: a whole 2x2x4 slice. The times are simulated.
32 devices in a mesh: row: 8 (over z, core), col: 4 (over y, x).
Axes of the slice: x: 2, y: 2, z: 4, core: 2. Of those that a mesh axis runs over, the one named last changes fastest.
Arguments:
- factor: bfloat16 [28672, 28672], P('row', 'col'), may hold values from -8 to 50
- subspace: bfloat16 [28672, 1024], P(('col', 'row')), may hold values from -6 to 6
Outputs:
- new_basis: float32 [28672, 1024], P(('row', 'col'))
- r_factor: float32 [1024, 1024], replicated
All inputs are finite; a program needn't handle non-finite values.
Results may differ from a plain program's by a relative error of at most 0.0009.
Values may be sent and summed in bfloat16 or wider, within the bound.
No kernel may reach another device: no remote copies, remote signals or barrier semaphores. Data moves between devices by JAX's collectives and lax.ppermute only.
A program may use at most 192 MiB of HBM per device.

v0:
```python
import functools

import jax
import jax.numpy as jnp
from jax import lax
from jax.experimental import pallas as pl
from jax.experimental.pallas import tpu as pltpu
from jax.sharding import PartitionSpec as P

WIDTHS = (512, 512)
COLUMN = 256
PIVOTS = 128
TILE = 8
BASE = (1, 1)
CORES = 2
ROW_TILE = 448
HIGHEST = lax.Precision.HIGHEST


class Timeline:
    def __init__(self):
        self.now = 0
        self.values = {}
        self.due = {}

    def put(self, key, value, at):
        self.values[key] = value
        self.due.setdefault(max(at, self.now + 1), []).append(key)

    def get(self, key):
        return self.values[key]

    def advance(self):
        self.now += 1
        keys = self.due.pop(self.now, [])
        passed = lax.optimization_barrier(tuple(self.values[k] for k in keys))
        self.values.update(zip(keys, passed))


def arrivals(levels):
    table = []
    for level in range(levels):
        came = []
        for step in range(1, levels):
            came += [("up", step)] if level >= step else []
            came += [("down", step)] if level + step < levels else []
        table.append(came)
    return table


def level_kernel(pieces, candidates, has_total, place_ref, factor_ref, *refs):
    blocks, (out_ref, panel_ref, sems) = refs[: 2 * candidates], refs[-3:]
    choice, core = place_ref[pieces + 1], place_ref[pieces + 2]
    rows = blocks[0].shape[0]

    @pl.when((pl.program_id(0) == 0) & (pl.program_id(1) == 0))
    def _():
        waits = []
        for swapped in range(2):
            start = pl.multiple_of(((1 - core) if swapped else core) * rows, 16)
            copies = [
                pltpu.make_async_copy(blocks[2 * k + swapped], panel_ref.at[pl.ds(start, rows)], sems.at[swapped])
                for k in range(candidates)
            ]
            for k, copy in enumerate(copies):

                @pl.when(choice == k)
                def _():
                    copy.start()

            waits.append(copies[0])
        for wait in waits:
            wait.wait()

    value = jnp.dot(factor_ref[...], panel_ref[...], preferred_element_type=jnp.float32)
    out_ref[0] = value + refs[2 * candidates][0] if has_total else value


def level_product(factor, blocks, total, place, part, rows):
    low, high = part
    pieces = high - low
    tile = rows
    while tile > ROW_TILE:
        tile //= 2
    per = rows // tile
    depth = CORES * rows
    width = blocks[0].shape[1]
    totals = [] if total is None else [total]
    whole = total is not None and total.shape[0] == pieces
    return pl.pallas_call(
        functools.partial(level_kernel, pieces, len(blocks) // 2, bool(totals)),
        out_shape=jax.ShapeDtypeStruct((pieces, rows, width), jnp.float32),
        grid_spec=pltpu.PrefetchScalarGridSpec(
            num_scalar_prefetch=1,
            grid=(pieces, per),
            in_specs=[pl.BlockSpec((tile, depth), lambda p, t, place: (place[p] * per + t, place[pieces]))]
            + [pl.BlockSpec(memory_space=pl.ANY)] * len(blocks)
            + [pl.BlockSpec((1, tile, width), lambda p, t, place: (p + low, t, 0))] * len(totals),
            out_specs=pl.BlockSpec((1, tile, width), lambda p, t, place: (p, t, 0)),
            scratch_shapes=[
                pltpu.VMEM((depth, width), factor.dtype),
                pltpu.SemaphoreType.DMA((2,)),
            ],
        ),
        input_output_aliases={2 + len(blocks): 0} if whole else {},
        compiler_params=pltpu.CompilerParams(vmem_limit_bytes=24 * 1024 * 1024),
        cost_estimate=pl.CostEstimate(
            flops=2 * pieces * rows * depth * width, bytes_accessed=2 * pieces * rows * depth, transcendentals=0
        ),
    )(place, factor, *blocks, *totals)


def product_kernel(levels, pieces, place_ref, factor_ref, *refs):
    blocks, (out_ref, panel_ref, sems) = refs[:-3], refs[-3:]
    level, core = place_ref[pieces], place_ref[pieces + 1]
    rows = blocks[0].shape[0]
    own, rising, falling = blocks[:2], blocks[2 : 2 * levels], blocks[2 * levels :]

    @pl.when((pl.program_id(0) == 0) & (pl.program_id(1) == 0))
    def _():
        def copy(block, slot, sem):
            start = pl.multiple_of(slot * rows, 16)
            return pltpu.make_async_copy(block, panel_ref.at[pl.ds(start, rows)], sems.at[sem])

        waits = []
        for swapped in range(2):
            at_core = (1 - core) if swapped else core
            first = copy(own[swapped], level * CORES + at_core, swapped)
            first.start()
            waits.append(first)
            for step in range(1, levels):
                slot = (level - step + levels) % levels * CORES + at_core
                sem = 2 * step + swapped
                below = copy(rising[2 * (step - 1) + swapped], slot, sem)
                above = copy(falling[2 * (levels - step - 1) + swapped], slot, sem)

                @pl.when(level >= step)
                def _():
                    below.start()

                @pl.when(level < step)
                def _():
                    above.start()

                waits.append(below)
        for wait in waits:
            wait.wait()

    out_ref[0] = jnp.dot(factor_ref[...], panel_ref[...], preferred_element_type=jnp.float32)


def product(factor, blocks, levels, place, pieces, rows):
    tile = rows
    while tile > ROW_TILE:
        tile //= 2
    per = rows // tile
    depth = factor.shape[1]
    width = blocks[0].shape[1]
    return pl.pallas_call(
        functools.partial(product_kernel, levels, pieces),
        out_shape=jax.ShapeDtypeStruct((pieces, rows, width), jnp.float32),
        grid_spec=pltpu.PrefetchScalarGridSpec(
            num_scalar_prefetch=1,
            grid=(pieces, per),
            in_specs=[pl.BlockSpec((tile, depth), lambda p, t, place: (place[p] * per + t, 0))]
            + [pl.BlockSpec(memory_space=pl.ANY)] * len(blocks),
            out_specs=pl.BlockSpec((1, tile, width), lambda p, t, place: (p, t, 0)),
            scratch_shapes=[
                pltpu.VMEM((depth, width), factor.dtype),
                pltpu.SemaphoreType.DMA((2 * levels,)),
            ],
        ),
        compiler_params=pltpu.CompilerParams(vmem_limit_bytes=30 * 1024 * 1024),
        cost_estimate=pl.CostEstimate(
            flops=2 * pieces * rows * depth * width, bytes_accessed=2 * pieces * rows * depth, transcendentals=0
        ),
    )(place, factor, *blocks)


def encode(piece):
    top = jnp.max(jnp.abs(piece), axis=0, keepdims=True)
    power = jnp.ceil(jnp.log2(jnp.maximum(top, 1e-30)))
    coded = (piece * jnp.exp2(14.0 - power)).astype(jnp.float16)
    tail = jnp.broadcast_to(power, (16, piece.shape[1])).astype(jnp.float16)
    return jnp.concatenate([coded, tail], axis=0)


def decode(sent):
    sent = sent.astype(jnp.float32)
    rows = sent.shape[0] - 16
    return sent[:rows] * jnp.exp2(sent[rows : rows + 1] - 14.0)


def inverse_of(x):
    guess = pl.reciprocal(x, approx=True)
    return guess * (2.0 - x * guess)


def eliminate(block):
    groups = PIVOTS // TILE
    shape = (TILE, PIVOTS)
    lane = lax.broadcasted_iota(jnp.int32, shape, 1)
    sub = lax.broadcasted_iota(jnp.int32, shape, 0)
    held = [block[g * TILE : (g + 1) * TILE] for g in range(groups)]
    factor, inverse = [], []
    for g in range(groups):
        base = g * TILE
        inside = (lane >= base) & (lane < base + TILE)
        rows = [jnp.broadcast_to(held[g][i : i + 1], shape) for i in range(TILE)]
        entry = [
            [jnp.broadcast_to(rows[i][:, base + j : base + j + 1], shape) if j >= i else None for j in range(TILE)]
            for i in range(TILE)
        ]
        upper = list(rows)
        unit = [jnp.where(inside, jnp.where(lane == base + i, 1.0, 0.0), rows[i]) for i in range(TILE)]
        pivot_inverse = []
        lower = [[None] * TILE for _ in range(TILE)]
        for k in range(TILE):
            pivot_inverse.append(inverse_of(entry[k][k]))
            for i in range(k + 1, TILE):
                weight = entry[k][i] * pivot_inverse[k]
                lower[i][k] = weight
                for j in range(i, TILE):
                    entry[i][j] = entry[i][j] - weight * entry[k][j]
                upper[i] = upper[i] - weight * upper[k]
                unit[i] = unit[i] - weight * unit[k]
        solved = [None] * TILE
        for k in reversed(range(TILE)):
            value = unit[k] * pivot_inverse[k]
            for i in range(k + 1, TILE):
                value = value - lower[i][k] * solved[i]
            solved[k] = value
        for h in range(g + 1, groups):
            old = held[h]
            new = jnp.where(inside, 0.0, old)
            for k in range(TILE):
                new = new - jnp.broadcast_to(old[:, base + k : base + k + 1], shape) * solved[k]
            held[h] = new
        diagonal, top, low = entry[0][0], upper[0], unit[0]
        for k in range(1, TILE):
            diagonal = jnp.where(sub == k, entry[k][k], diagonal)
            top = jnp.where(sub == k, upper[k], top)
            low = jnp.where(sub == k, unit[k], low)
        root = lax.rsqrt(diagonal)
        root = root * (1.5 - 0.5 * diagonal * root * root)
        own = sub + base
        factor.append(jnp.where(lane >= own, top * root, 0.0))
        inverse.append(jnp.where(lane <= own, low * root, 0.0))
    return jnp.concatenate(factor, 0), jnp.concatenate(inverse, 0)


def mul(a, b):
    return jnp.dot(a, b, precision=HIGHEST, preferred_element_type=jnp.float32)


def column_kernel(scale, before, width, gram_ref, *refs):
    factor_ref, inverse_ref = refs[-2:]
    block = gram_ref[before:, :] * scale
    if before:
        above = mul(refs[0][...], gram_ref[:before, :] * scale)
        factor_ref[:before, :] = above
        above_t = above.T
        block = block - mul(above_t, above)
    block = (block + block.T) * 0.5
    if width == PIVOTS:
        factor, inverse = eliminate(block)
    else:
        first, first_inverse = eliminate(block[:PIVOTS, :PIVOTS])
        corner = mul(first_inverse, block[:PIVOTS, PIVOTS:])
        corner_t = corner.T
        last, last_inverse = eliminate(block[PIVOTS:, PIVOTS:] - mul(corner_t, corner))
        low = -mul(last_inverse, mul(corner_t, first_inverse))
        none = jnp.zeros((PIVOTS, PIVOTS), jnp.float32)
        factor = jnp.concatenate(
            [jnp.concatenate([first, corner], 1), jnp.concatenate([none, last], 1)], 0
        )
        inverse = jnp.concatenate(
            [jnp.concatenate([first_inverse, none], 1), jnp.concatenate([low, last_inverse], 1)], 0
        )
    factor_ref[before:, :] = factor
    inverse_ref[:, before:] = inverse
    if before:
        inverse_ref[:, :before] = -mul(mul(inverse, above_t), refs[0][...])


def factor_column(gram, inverse_before, scale):
    width = gram.shape[1]
    before = gram.shape[0] - width
    operands = (gram,) if inverse_before is None else (gram, inverse_before)
    return pl.pallas_call(
        functools.partial(column_kernel, scale, before, width),
        out_shape=(
            jax.ShapeDtypeStruct((before + width, width), jnp.float32),
            jax.ShapeDtypeStruct((width, before + width), jnp.float32),
        ),
        in_specs=[pl.BlockSpec(memory_space=pltpu.VMEM)] * len(operands),
        out_specs=(pl.BlockSpec(memory_space=pltpu.VMEM),) * 2,
        compiler_params=pltpu.CompilerParams(vmem_limit_bytes=32 * 1024 * 1024),
        cost_estimate=pl.CostEstimate(flops=16_000_000_000, bytes_accessed=4_000_000, transcendentals=0),
    )(*operands)


def body(row_size, col_size, factor, subspace):
    rows = subspace.shape[0]
    total_rows = rows * row_size * col_size
    levels = row_size // CORES
    chunks = len(WIDTHS)
    starts = [sum(WIDTHS[:c]) for c in range(chunks)]
    row, col = lax.axis_index("row"), lax.axis_index("col")
    level, core = row // CORES, row % CORES
    up = [(i, i + CORES) for i in range(row_size - CORES)]
    down = [(i + CORES, i) for i in range(row_size - CORES)]
    swap = [(i, i // CORES * CORES + (i + 1) % CORES) for i in range(row_size)]

    line = Timeline()
    put, get = line.put, line.get
    tasks = {}

    def at(slot, task):
        tasks.setdefault(slot, []).append(task)

    sent = {(c, step): c * (levels - 2) + step - 1 for c in range(chunks) for step in range(1, levels)}
    arrival = {key: slot + 1 for key, slot in sent.items()}

    def send_line(c, step):
        def task():
            for way, perm in (("up", up), ("down", down)):
                source = get((way, c, step - 1)) if step > 1 else get(("own", c))
                put((way, c, step), lax.ppermute(source, "row", perm), arrival[c, step])

        return task

    def swap_cores(c, step):
        def task():
            for key in [("up", c, step), ("down", c, step)] if step else [("own", c)]:
                line.values[("swap",) + key] = lax.ppermute(get(key), "row", swap)

        return task

    for c, width in enumerate(WIDTHS):
        own = lax.slice_in_dim(subspace, starts[c], starts[c] + width, axis=1)
        put(("own", c), own, sent[c, 1])
        at(sent[c, 1], swap_cores(c, 0))
        for step in range(1, levels):
            at(sent[c, step], send_line(c, step))
            at(arrival[c, step], swap_cores(c, step))

    def parts_of(c):
        calls = min(1 if c < chunks - 1 else 2, col_size)
        return [(col_size * i // calls, col_size * (i + 1) // calls) for i in range(calls)]

    def assemble(c):
        def task():
            blocks = [get(("own", c)), get(("swap", "own", c))]
            for way in ("up", "down"):
                for step in range(1, levels):
                    blocks += [get((way, c, step)), get(("swap", way, c, step))]
            line.values["blocks", c] = blocks

        return task

    split = factor.shape[1] // levels % 128 == 0
    table = arrivals(levels)

    def pick(values, dtype=jnp.int32):
        return lax.dynamic_index_in_dim(jnp.array(values, dtype), level, 0, keepdims=False)

    def place_of(part, window):
        if window is None:
            scalars = [level, core]
        elif window == 0:
            scalars = [level, jnp.zeros_like(level), core]
        else:
            came = [ways[window - 1] for ways in table]
            source = [i + (step if way == "down" else -step) for i, (way, step) in enumerate(came)]
            choice = [2 * (step - 1) + (way == "down") for way, step in came]
            scalars = [pick(source), pick(choice), core]
        return jnp.stack([(col + 1 + p) % col_size for p in range(*part)] + scalars).astype(jnp.int32)

    def multiply(c, part, window):
        def task():
            place = get(("place", c, part, window))
            if window is None:
                value = product(factor, get(("blocks", c)), levels, place, part[1] - part[0], rows)
            else:
                keys = [("own", c)] if window == 0 else []
                for step in range(1, window + 1):
                    keys += [("up", c, step), ("down", c, step)]
                blocks = []
                for key in keys:
                    blocks += [get(key), get(("swap",) + key)]
                total = line.values.get(("total", c))
                value = level_product(factor, blocks, total, place, part, rows)
            if window is None or window == levels - 1:
                line.values["product", c, part] = value
            else:
                put(("total", c), value, line.now + 1)

        return task

    def send_pieces(c, part, due):
        def task():
            value = get(("product", c, part))
            for p in range(*part):
                piece = value[p - part[0]]
                if p == col_size - 1:
                    line.values["kept", c] = piece
                else:
                    perm = [(i, (i + p + 1) % col_size) for i in range(col_size)]
                    coded = encode(piece)
                    put(("coded", c, p), coded, line.now + 1)
                    put(("got", c, p), lax.ppermute(coded, "col", perm), due)

        return task

    def add_pieces(c):
        def task():
            total = get(("kept", c))
            for p in range(col_size - 1):
                total = total + decode(get(("got", c, p)))
            line.values["image", c] = total
            images = [get(("image", i)) for i in range(c + 1)]
            line.values["so far", c] = jnp.concatenate(images, axis=1) if c else total

        return task

    stages = (
        ("row", CORES, core, lambda step: [(i, i // CORES * CORES + (i + step) % CORES) for i in range(row_size)]),
        ("col", col_size, col, lambda step: [(i, (i + step) % col_size) for i in range(col_size)]),
        ("row", levels, level, lambda step: [(i, (i + step * CORES) % row_size) for i in range(row_size)]),
    )

    def inner_products(c):
        def task():
            line.values["sum", c] = lax.dot_general(
                get(("so far", c)),
                get(("image", c)),
                (((0,), (0,)), ((), ())),
                precision=HIGHEST,
                preferred_element_type=jnp.float32,
            )

        return task

    def scatter_send(c, stage):
        def task():
            axis, size, index, perm = stages[stage]
            block = get(("sum", c))
            part = block.shape[0] // size
            for step in range(1, size):
                piece = lax.dynamic_slice_in_dim(block, (index + step) % size * part, part, 0)
                put(("add", c, step), lax.ppermute(piece, axis, perm(step)), line.now + 1)

        return task

    def scatter_add(c, stage):
        def task():
            _, size, index, _ = stages[stage]
            block = get(("sum", c))
            part = block.shape[0] // size
            total = lax.dynamic_slice_in_dim(block, index * part, part, 0)
            for step in range(1, size):
                total = total + get(("add", c, step))
            line.values["sum", c] = total

        return task

    def gather_send(c, stage):
        def task():
            axis, size, _, perm = stages[stage]
            for step in range(1, size):
                put(("add", c, step), lax.ppermute(get(("sum", c)), axis, perm(step)), line.now + 1)

        return task

    def gather_put(c, stage):
        def task():
            _, size, index, _ = stages[stage]
            block = get(("sum", c))
            part = block.shape[0]
            whole = jnp.zeros((size * part, block.shape[1]), block.dtype)
            whole = lax.dynamic_update_slice_in_dim(whole, block, index * part, 0)
            for step in range(1, size):
                whole = lax.dynamic_update_slice_in_dim(
                    whole, get(("add", c, step)), (index - step + size) % size * part, 0
                )
            line.values["sum", c] = whole

        return task


    def finish(c):
        def task():
            gram, inverse = get(("sum", c)), line.values.get("inverse")
            for low in range(0, WIDTHS[c], COLUMN):
                end = starts[c] + low + COLUMN
                column, last_rows = factor_column(gram[:end, low : low + COLUMN], inverse, 1.0 / total_rows)
                line.values["column", end] = jnp.pad(column, ((0, subspace.shape[1] - end), (0, 0)))
                if inverse is None:
                    inverse = last_rows
                else:
                    inverse = jnp.concatenate([jnp.pad(inverse, ((0, 0), (0, COLUMN))), last_rows], axis=0)
            line.values["inverse"] = inverse
            put(("last", c), inverse[starts[c] :], line.now + 1)

        return task

    def multiply_basis(c):
        def task():
            line.values["basis", c] = lax.dot_general(
                get(("so far", c)),
                get(("last", c)),
                (((1,), (1,)), ((), ())),
                precision=lax.Precision.HIGH,
                preferred_element_type=jnp.float32,
            )

        return task

    busy = 0
    for c in range(chunks):
        ready = max(arrival[c, levels - 1], busy)
        at(ready, assemble(c))
        everything = (0, col_size)
        for window in range(levels - 1 if split else 0):
            slot = sent[c, 1] if window == 0 else arrival[c, window]
            if c and window:
                slot = max(slot, arrival[c - 1, levels - 1] + 1)
            put(("place", c, everything, window), place_of(everything, window), slot)
            at(slot, multiply(c, everything, window))
        parts = parts_of(c)
        window = levels - 1 if split else None
        for i, part in enumerate(parts):
            put(("place", c, part, window), place_of(part, window), ready + i)
            at(ready + i, multiply(c, part, window))
        busy = ready + len(parts)
        slot = BASE[c] + busy
        for i, part in enumerate(parts):
            at(ready + i, send_pieces(c, part, slot))
        at(slot, add_pieces(c))
        at(slot, inner_products(c))
        for stage in range(len(stages)):
            at(slot, scatter_send(c, stage))
            at(slot + 1, scatter_add(c, stage))
            slot += 1
        for stage in reversed(range(len(stages))):
            at(slot, gather_send(c, stage))
            at(slot + 1, gather_put(c, stage))
            slot += 1
        at(slot, finish(c))
        at(slot + 1, multiply_basis(c))

    for slot in range(max(tasks) + 1):
        if slot:
            line.advance()
        for task in tasks.get(slot, []):
            task()
    basis = jnp.concatenate([get(("basis", c)) for c in range(chunks)], axis=1)
    upper = jnp.concatenate(
        [get(("column", end)) for end in range(COLUMN, subspace.shape[1] + 1, COLUMN)], axis=1
    )
    return basis, upper


def solution(mesh):
    row_size, col_size = mesh.shape["row"], mesh.shape["col"]
    return jax.shard_map(
        functools.partial(body, row_size, col_size),
        mesh=mesh,
        in_specs=(P("row", "col"), P(("col", "row"), None)),
        out_specs=(P(("row", "col"), None), P()),
        check_vma=False,
    )
```

profile of v0, /device:TPU:1, one launch (start us, length us, event | category | flops | bytes accessed | tf_op | source)
XLA Modules:
  0.0 430.0 jit_solution(17604530519564703966)
XLA Ops:
  0.7 2.5 fusion.31
  3.2 4.7 %collective-permute-start = (bf16[896,512]{1,0:T(8,128)(2,1)S(1)}, bf16[896,512]{1,0:T(8,128)(2,1)S(1)}, u32[]{:S(2)}, u32[]{:S(2)}) collective-permute-start(bf16[896,512]{1,0:T(8,128)(2,1)S(1)} %get-tuple-element.154.refs_0_), channel_id=1, source_target_pairs={{0,8},{4,12},{8,16},{12,20},{16,24},{20,28},{1,9},{5,13},{9,17},{1... | collective-permute-start | bytes 2752520 | tf_op jit(solution)/shard_map/ppermute | solution.py:329
  11.9 13.0 %shard_map.167.refs_4_ = f32[4,896,512]{2,1,0:T(8,128)S(1)} custom-call(s32[7]{0:T(128)S(1)} %stack.36.place_ref, bf16[3584,7168]{1,0:T(8,128)(2,1)} %factor_ref.17, bf16[896,512]{1,0:T(8,128)(2,1)S(1)} %get-tuple-element.154.refs_0_, bf16[896,512]{1,0:T(8,128)(2,1)} %collective-permute-done.2.refs_1_), custom_call_target="tpu_custom_call" | custom-call | flops 6576668672 | bytes 12845056 | tf_op jit(solution)/shard_map/pallas_call | solution.py:90
  25.0 2.9 copy-done
  27.9 3.6 collective-permute-done.1.refs_2_
  32.6 4.1 collective-permute-start.3
  40.5 3.4 copy-done.1
  43.9 13.1 %shard_map.168.refs_8_ = f32[4,896,512]{2,1,0:T(8,128)S(1)} custom-call(s32[7]{0:T(128)S(1)} %stack.37.place_ref, bf16[3584,7168]{1,0:T(8,128)(2,1)} %factor_ref.17, bf16[896,512]{1,0:T(8,128)(2,1)S(1)} %collective-permute-done.refs_0_, bf16[896,512]{1,0:T(8,128)(2,1)S(1)} %collective-permute-done.5.refs_1_, ...), custom_call_target="tpu_custom_call", output_to_operand_aliasing={{}: (6, {})} | custom-call | flops 6576668672 | bytes 12845056 | tf_op jit(solution)/shard_map/pallas_call | solution.py:90
  57.1 2.9 copy-done.2
  60.0 1.4 collective-permute-start.13
  65.9 4.0 collective-permute-start.7
  72.2 4.0 collective-permute-start.9
  76.3 14.1 %shard_map.170.refs_4_ = f32[4,896,512]{2,1,0:T(8,128)S(1)} custom-call(s32[7]{0:T(128)S(1)} %stack.36.place_ref, bf16[3584,7168]{1,0:T(8,128)(2,1)} %factor_ref.17, bf16[896,512]{1,0:T(8,128)(2,1)} %get-tuple-element.76.refs_0_, bf16[896,512]{1,0:T(8,128)(2,1)} %collective-permute-done.13.refs_1_), custom_call_target="tpu_custom_call" | custom-call | flops 6576668672 | bytes 12845056 | tf_op jit(solution)/shard_map/pallas_call | solution.py:90
  90.5 2.9 copy-done.5
  93.4 13.2 %shard_map.169.refs_12_ = f32[4,896,512]{2,1,0:T(8,128)S(1)} custom-call(s32[7]{0:T(128)S(1)} %stack.34.place_ref, bf16[3584,7168]{1,0:T(8,128)(2,1)} %factor_ref.17, bf16[896,512]{1,0:T(8,128)(2,1)S(1)} %collective-permute-done.refs_0_, bf16[896,512]{1,0:T(8,128)(2,1)S(1)} %copy-done.15, ...), custom_call_target="tpu_custom_call", output_to_operand_aliasing={{}: (10, {})} | custom-call | flops 6576668672 | bytes 12845056 | tf_op jit(solution)/shard_map/pallas_call | solution.py:90
  106.7 1.7 collective-permute-done.8.refs_10_
  110.5 4.9 %collective-permute-start.19 = (bf16[896,512]{1,0:T(8,128)(2,1)S(1)}, bf16[896,512]{1,0:T(8,128)(2,1)}, u32[]{:S(2)}, u32[]{:S(2)}) collective-permute-start(bf16[896,512]{1,0:T(8,128)(2,1)S(1)} %collective-permute-done.9.refs_0_), channel_id=1, source_target_pairs={{0,8},{4,12},{8,16},{12,20},{16,24},{20,28},{1,9},{5,13},{9,17},{1... | collective-permute-start | bytes 2752520 | tf_op jit(solution)/shard_map/ppermute | solution.py:329
  118.8 12.1 %shard_map.171 = f32[4,896,512]{2,1,0:T(8,128)S(1)} custom-call(s32[7]{0:T(128)S(1)} %stack.33.place_ref, bf16[3584,7168]{1,0:T(8,128)(2,1)} %factor_ref.17, bf16[896,512]{1,0:T(8,128)(2,1)S(1)} %copy-done.11, bf16[896,512]{1,0:T(8,128)(2,1)S(1)} %copy-done.15, bf16[896,512]{1,0:T(8,128)(2,1)S(1)} %copy-done.13, ...), custom_call_target="tpu_custom_call", output_to_operand_aliasing={{}: (14, {})} | custom-call | flops 6576668672 | bytes 12845056 | tf_op jit(solution)/shard_map/pallas_call | solution.py:90
  132.3 1.6 copy-done.4
  137.4 2.8 collective-permute-done.20.refs_6_
  143.6 2.3 collective-permute-start.21
  147.2 2.2 collective-permute-start.18
  150.4 3.1 copy-done.6
  153.5 13.1 %shard_map.172.refs_8_ = f32[4,896,512]{2,1,0:T(8,128)S(1)} custom-call(s32[7]{0:T(128)S(1)} %stack.37.place_ref, bf16[3584,7168]{1,0:T(8,128)(2,1)} %factor_ref.17, bf16[896,512]{1,0:T(8,128)(2,1)S(1)} %collective-permute-done.9.refs_0_, bf16[896,512]{1,0:T(8,128)(2,1)S(1)} %collective-permute-done.23.refs_1_, ...), custom_call_target="tpu_custom_call", output_to_operand_aliasing={{}: (6, {})} | custom-call | flops 6576668672 | bytes 12845056 | tf_op jit(solution)/shard_map/pallas_call | solution.py:90
  166.6 13.2 %shard_map.173.refs_12_ = f32[4,896,512]{2,1,0:T(8,128)S(1)} custom-call(s32[7]{0:T(128)S(1)} %stack.34.place_ref, bf16[3584,7168]{1,0:T(8,128)(2,1)} %factor_ref.17, bf16[896,512]{1,0:T(8,128)(2,1)S(1)} %collective-permute-done.9.refs_0_, bf16[896,512]{1,0:T(8,128)(2,1)S(1)} %collective-permute-done.23.refs_1_, ...), custom_call_target="tpu_custom_call", output_to_operand_aliasing={{}: (10, {})} | custom-call | flops 6576668672 | bytes 12845056 | tf_op jit(solution)/shard_map/pallas_call | solution.py:90
  179.8 2.9 copy-done.7
  182.8 7.5 %collective-permute-done.16 = f16[912,512]{1,0:T(8,128)(2,1)S(1)} collective-permute-done((f16[912,512]{1,0:T(8,128)(2,1)}, f16[912,512]{1,0:T(8,128)(2,1)S(1)}, u32[]{:S(2)}, u32[]{:S(2)}) %collective-permute-start.16) | collective-permute-done | bytes 933920 | tf_op jit(solution)/shard_map/ppermute | solution.py:412
  191.1 2.6 collective-permute-start.28
  193.8 2.6 fusion.8
  196.4 3.5 fusion.32
  200.5 7.1 %shard_map.174 = f32[2,896,512]{2,1,0:T(8,128)S(1)} custom-call(s32[5]{0:T(128)S(1)} %stack.38.place_ref, bf16[3584,7168]{1,0:T(8,128)(2,1)} %factor_ref.17, bf16[896,512]{1,0:T(8,128)(2,1)S(1)} %collective-permute-done.9.refs_0_, bf16[896,512]{1,0:T(8,128)(2,1)S(1)} %collective-permute-done.23.refs_1_, ...), custom_call_target="tpu_custom_call" | custom-call | flops 3288334336 | bytes 6422528 | tf_op jit(solution)/shard_map/pallas_call | solution.py:90
  211.3 7.1 %shard_map.175 = f32[2,896,512]{2,1,0:T(8,128)S(1)} custom-call(s32[5]{0:T(128)S(1)} %stack.41.place_ref, bf16[3584,7168]{1,0:T(8,128)(2,1)} %factor_ref.17, bf16[896,512]{1,0:T(8,128)(2,1)S(1)} %collective-permute-done.9.refs_0_, bf16[896,512]{1,0:T(8,128)(2,1)S(1)} %collective-permute-done.23.refs_1_, ...), custom_call_target="tpu_custom_call" | custom-call | flops 3288334336 | bytes 6422528 | tf_op jit(solution)/shard_map/pallas_call | solution.py:90
  218.8 1.5 copy-done.8
  220.5 2.1 collective-permute-start.35
  224.1 32.9 %collective-permute-done.30 = f32[64,512]{1,0:T(8,128)S(1)} collective-permute-done((f32[64,512]{1,0:T(8,128)S(1)}, f32[64,512]{1,0:T(8,128)S(1)}, u32[]{:S(2)}, u32[]{:S(2)}) %collective-permute-start.30) | collective-permute-done | bytes 131104 | tf_op jit(solution)/shard_map/ppermute | solution.py:452
  257.0 3.8 collective-permute-done.32
  260.9 3.2 collective-permute-start.36
  264.0 1.4 collective-permute-done.36
  266.4 1.5 collective-permute-done.37
  270.2 1.6 convert_element_type.88
  274.0 6.7 %fusion.4 = f32[1024,512]{1,0:T(8,128)S(1)} fusion(f32[896,512]{1,0:T(8,128)S(1)} %fusion.5, f32[896,512]{1,0:T(8,128)S(1)} %copy-done.19), kind=kOutput, calls=%fused_computation.12 | convolution fusion | flops 5638062080 | bytes 5767168 | tf_op jit(solution)/shard_map/dot_general | solution.py:435
  282.0 4.4 %collective-permute-start.42 = (f32[512,512]{1,0:T(8,128)S(1)}, f32[512,512]{1,0:T(8,128)}, u32[]{:S(2)}, u32[]{:S(2)}) collective-permute-start(f32[512,512]{1,0:T(8,128)S(1)} %constant_dynamic-slice_fusion.6), channel_id=1, source_target_pairs={{0,4},{4,0},{8,12},{12,8},{16,20},{20,16},{24,28},{28,24},{1,5},{5... | collective-permute-start | bytes 3145736 | tf_op jit(solution)/shard_map/ppermute | solution.py:452
  291.1 2.0 collective-permute-done.40
  293.1 1.8 dynamic-slice_add_fusion
  295.6 1.8 collective-permute-start.43
  299.5 6.2 %collective-permute-done.43 = f32[64,512]{1,0:T(8,128)S(1)} collective-permute-done((f32[64,512]{1,0:T(8,128)S(1)}, f32[64,512]{1,0:T(8,128)S(1)}, u32[]{:S(2)}, u32[]{:S(2)}) %collective-permute-start.43) | collective-permute-done | bytes 131104 | tf_op jit(solution)/shard_map/ppermute | solution.py:472
  305.8 9.5 %collective-permute-done.44 = f32[64,512]{1,0:T(8,128)S(1)} collective-permute-done((f32[64,512]{1,0:T(8,128)S(1)}, f32[64,512]{1,0:T(8,128)S(1)}, u32[]{:S(2)}, u32[]{:S(2)}) %collective-permute-start.44) | collective-permute-done | bytes 131104 | tf_op jit(solution)/shard_map/ppermute | solution.py:472
  318.4 1.5 collective-permute-start.51
  321.4 2.1 collective-permute-done.50
  323.5 2.0 collective-permute-done.51
  326.8 1.8 collective-permute-start.53
  328.6 1.5 collective-permute-start.54
  331.1 12.4 %shard_map.176 = (f32[256,256]{1,0:T(8,128)S(1)}, f32[256,256]{1,0:T(8,128)S(1)}) custom-call(f32[256,256]{1,0:T(8,128)S(1)} %slice.128.gram_ref), custom_call_target="tpu_custom_call" | custom-call | flops 16000000000 | bytes 4000000 | tf_op jit(solution)/shard_map/pallas_call | solution.py:290
  343.6 14.6 %shard_map.177 = (f32[512,256]{1,0:T(8,128)S(1)}, f32[256,512]{1,0:T(8,128)S(1)}) custom-call(f32[512,256]{1,0:T(8,128)S(1)} %slice.129.gram_ref, f32[256,256]{1,0:T(8,128)S(1)} %get-tuple-element.120.refs_0_), custom_call_target="tpu_custom_call" | custom-call | flops 16000000000 | bytes 4000000 | tf_op jit(solution)/shard_map/pallas_call | solution.py:290
  358.4 1.6 collective-permute-start.56
  362.1 3.6 collective-permute-done.56
  365.7 7.5 %collective-permute-done.57 = f32[128,512]{1,0:T(8,128)S(1)} collective-permute-done((f32[128,512]{1,0:T(8,128)S(1)}, f32[128,512]{1,0:T(8,128)S(1)}, u32[]{:S(2)}, u32[]{:S(2)}) %collective-permute-start.57) | collective-permute-done | bytes 262176 | tf_op jit(solution)/shard_map/ppermute | solution.py:472
  373.9 1.8 fusion.33
  376.4 16.7 %shard_map.178 = (f32[768,256]{1,0:T(8,128)S(1)}, f32[256,768]{1,0:T(8,128)S(1)}) custom-call(f32[768,256]{1,0:T(8,128)S(1)} %slice.130.gram_ref, f32[512,512]{1,0:T(8,128)S(1)} %select_maximum_fusion.3.refs_0_), custom_call_target="tpu_custom_call" | custom-call | flops 16000000000 | bytes 4000000 | tf_op jit(solution)/shard_map/pallas_call | solution.py:290
  393.3 21.2 %shard_map.179 = (f32[1024,256]{1,0:T(8,128)S(1)}, f32[256,1024]{1,0:T(8,128)S(1)}) custom-call(f32[1024,256]{1,0:T(8,128)S(1)} %slice.131.gram_ref, f32[768,768]{1,0:T(8,128)S(1)} %select_maximum_fusion.2.refs_0_), custom_call_target="tpu_custom_call" | custom-call | flops 16000000000 | bytes 4000000 | tf_op jit(solution)/shard_map/pallas_call | solution.py:290
  416.6 3.6 fusion.3
  420.1 2.1 pad_maximum_fusion.3
  422.2 5.0 %copy.23 = f32[896,1024]{1,0:T(8,128)} copy(f32[896,1024]{0,1:T(8,128)} %pad_maximum_fusion.3) | data formatting | bytes 7340032
  427.2 2.6 fusion
  (240 shorter events, 65.8 us)
Async XLA Ops:
  3.2 8.8 %collective-permute-start.2 = (bf16[896,512]{1,0:T(8,128)(2,1)S(1)}, bf16[896,512]{1,0:T(8,128)(2,1)}, u32[]{:S(2)}, u32[]{:S(2)}) collective-permute-start(bf16[896,512]{1,0:T(8,128)(2,1)S(1)} %get-tuple-element.154.refs_0_), channel_id=1, source_target_pairs={{0,4},{4,0},{8,12},{12,8},{16,20},{20,16},{24,28},{28,24},{1,5},{5... | collective-permute-start | bytes 2752520 | tf_op jit(solution)/shard_map/ppermute | solution.py:336
  3.2 24.7 %collective-permute-start = (bf16[896,512]{1,0:T(8,128)(2,1)S(1)}, bf16[896,512]{1,0:T(8,128)(2,1)S(1)}, u32[]{:S(2)}, u32[]{:S(2)}) collective-permute-start(bf16[896,512]{1,0:T(8,128)(2,1)S(1)} %get-tuple-element.154.refs_0_), channel_id=1, source_target_pairs={{0,8},{4,12},{8,16},{12,20},{16,24},{20,28},{1,9},{5,13},{9,17},{1... | collective-permute-start | bytes 2752520 | tf_op jit(solution)/shard_map/ppermute | solution.py:329
  7.9 23.6 %collective-permute-start.1 = (bf16[896,512]{1,0:T(8,128)(2,1)S(1)}, bf16[896,512]{1,0:T(8,128)(2,1)S(1)}, u32[]{:S(2)}, u32[]{:S(2)}) collective-permute-start(bf16[896,512]{1,0:T(8,128)(2,1)S(1)} %get-tuple-element.154.refs_0_), channel_id=1, source_target_pairs={{8,0},{12,4},{16,8},{20,12},{24,16},{28,20},{9,1},{13,5},{17,9},{2... | collective-permute-start | bytes 2752520 | tf_op jit(solution)/shard_map/ppermute | solution.py:329
  11.9 26.7 %copy-start.29 = (s32[4]{0:T(128)S(1)}, s32[4]{0:T(128)}, u32[]{:S(2)}) copy-start(s32[4]{0:T(128)} %constant.294.clone) | copy-start | bytes 52
  27.9 65.5 %copy-start.10 = (bf16[896,512]{1,0:T(8,128)(2,1)}, bf16[896,512]{1,0:T(8,128)(2,1)S(1)}, u32[]{:S(2)}) copy-start(bf16[896,512]{1,0:T(8,128)(2,1)S(1)} %collective-permute-done.refs_0_) | copy-start | bytes 2752516
  31.5 9.0 %collective-permute-start.5 = (bf16[896,512]{1,0:T(8,128)(2,1)S(1)}, bf16[896,512]{1,0:T(8,128)(2,1)S(1)}, u32[]{:S(2)}, u32[]{:S(2)}) collective-permute-start(bf16[896,512]{1,0:T(8,128)(2,1)S(1)} %collective-permute-done.refs_0_), channel_id=1, source_target_pairs={{0,4},{4,0},{8,12},{12,8},{16,20},{20,16},{24,28},{28,24},{1,5},{5... | collective-permute-start | bytes 2752520 | tf_op jit(solution)/shard_map/ppermute | solution.py:336
  32.6 7.9 %collective-permute-start.6 = (bf16[896,512]{1,0:T(8,128)(2,1)S(1)}, bf16[896,512]{1,0:T(8,128)(2,1)}, u32[]{:S(2)}, u32[]{:S(2)}) collective-permute-start(bf16[896,512]{1,0:T(8,128)(2,1)S(1)} %collective-permute-done.1.refs_2_), channel_id=1, source_target_pairs={{0,4},{4,0},{8,12},{12,8},{16,20},{20,16},{24,28},{28,24},{1,5},{5... | collective-permute-start | bytes 2752520 | tf_op jit(solution)/shard_map/ppermute | solution.py:336
  32.6 27.4 %collective-permute-start.3 = (bf16[896,512]{1,0:T(8,128)(2,1)S(1)}, bf16[896,512]{1,0:T(8,128)(2,1)}, u32[]{:S(2)}, u32[]{:S(2)}) collective-permute-start(bf16[896,512]{1,0:T(8,128)(2,1)S(1)} %collective-permute-done.refs_0_), channel_id=1, source_target_pairs={{0,8},{4,12},{8,16},{12,20},{16,24},{20,28},{1,9},{5,13},{9,17},{1... | collective-permute-start | bytes 2752520 | tf_op jit(solution)/shard_map/ppermute | solution.py:329
  36.7 23.3 %collective-permute-start.4 = (bf16[896,512]{1,0:T(8,128)(2,1)S(1)}, bf16[896,512]{1,0:T(8,128)(2,1)}, u32[]{:S(2)}, u32[]{:S(2)}) collective-permute-start(bf16[896,512]{1,0:T(8,128)(2,1)S(1)} %collective-permute-done.1.refs_2_), channel_id=1, source_target_pairs={{8,0},{12,4},{16,8},{20,12},{24,16},{28,20},{9,1},{13,5},{17,9},{2... | collective-permute-start | bytes 2752520 | tf_op jit(solution)/shard_map/ppermute | solution.py:329
  60.0 10.0 %collective-permute-start.13 = (bf16[896,512]{1,0:T(8,128)(2,1)}, bf16[896,512]{1,0:T(8,128)(2,1)}, u32[]{:S(2)}, u32[]{:S(2)}) collective-permute-start(bf16[896,512]{1,0:T(8,128)(2,1)} %get-tuple-element.76.refs_0_), channel_id=1, source_target_pairs={{0,4},{4,0},{8,12},{12,8},{16,20},{20,16},{24,28},{28,24},{1,5},{5... | collective-permute-start | bytes 2752520 | tf_op jit(solution)/shard_map/ppermute | solution.py:336
  61.4 9.9 %collective-permute-start.11 = (bf16[896,512]{1,0:T(8,128)(2,1)}, bf16[896,512]{1,0:T(8,128)(2,1)S(1)}, u32[]{:S(2)}, u32[]{:S(2)}) collective-permute-start(bf16[896,512]{1,0:T(8,128)(2,1)} %collective-permute-done.3.refs_4_), channel_id=1, source_target_pairs={{0,4},{4,0},{8,12},{12,8},{16,20},{20,16},{24,28},{28,24},{1,5},{5... | collective-permute-start | bytes 2752520 | tf_op jit(solution)/shard_map/ppermute | solution.py:336
  61.4 32.0 %collective-permute-start.12 = (bf16[896,512]{1,0:T(8,128)(2,1)}, bf16[896,512]{1,0:T(8,128)(2,1)}, u32[]{:S(2)}, u32[]{:S(2)}) collective-permute-start(bf16[896,512]{1,0:T(8,128)(2,1)} %collective-permute-done.4.refs_6_), channel_id=1, source_target_pairs={{0,4},{4,0},{8,12},{12,8},{16,20},{20,16},{24,28},{28,24},{1,5},{5... | collective-permute-start | bytes 2752520 | tf_op jit(solution)/shard_map/ppermute | solution.py:336
  64.5 28.9 %copy-start.13 = (bf16[896,512]{1,0:T(8,128)(2,1)S(1)}, bf16[896,512]{1,0:T(8,128)(2,1)}, u32[]{:S(2)}) copy-start(bf16[896,512]{1,0:T(8,128)(2,1)} %copy-done.12) | copy-start | bytes 2752516
  64.5 28.9 %copy-start.15 = (bf16[896,512]{1,0:T(8,128)(2,1)S(1)}, bf16[896,512]{1,0:T(8,128)(2,1)}, u32[]{:S(2)}) copy-start(bf16[896,512]{1,0:T(8,128)(2,1)} %copy-done.14) | copy-start | bytes 2752516
  64.5 42.1 %collective-permute-start.10 = (bf16[896,512]{1,0:T(8,128)(2,1)}, bf16[896,512]{1,0:T(8,128)(2,1)S(1)}, u32[]{:S(2)}, u32[]{:S(2)}) collective-permute-start(bf16[896,512]{1,0:T(8,128)(2,1)} %get-tuple-element.76.refs_0_), channel_id=1, source_target_pairs={{8,0},{12,4},{16,8},{20,12},{24,16},{28,20},{9,1},{13,5},{17,9},{2... | collective-permute-start | bytes 2752520 | tf_op jit(solution)/shard_map/ppermute | solution.py:329
  65.9 40.7 %collective-permute-start.7 = (bf16[896,512]{1,0:T(8,128)(2,1)}, bf16[896,512]{1,0:T(8,128)(2,1)S(1)}, u32[]{:S(2)}, u32[]{:S(2)}) collective-permute-start(bf16[896,512]{1,0:T(8,128)(2,1)} %collective-permute-done.3.refs_4_), channel_id=1, source_target_pairs={{0,8},{4,12},{8,16},{12,20},{16,24},{20,28},{1,9},{5,13},{9,17},{1... | collective-permute-start | bytes 2752520 | tf_op jit(solution)/shard_map/ppermute | solution.py:329
  70.0 38.4 %collective-permute-start.8 = (bf16[896,512]{1,0:T(8,128)(2,1)}, bf16[896,512]{1,0:T(8,128)(2,1)S(1)}, u32[]{:S(2)}, u32[]{:S(2)}) collective-permute-start(bf16[896,512]{1,0:T(8,128)(2,1)} %collective-permute-done.4.refs_6_), channel_id=1, source_target_pairs={{8,0},{12,4},{16,8},{20,12},{24,16},{28,20},{9,1},{13,5},{17,9},{2... | collective-permute-start | bytes 2752520 | tf_op jit(solution)/shard_map/ppermute | solution.py:329
  72.2 37.1 %collective-permute-start.9 = (bf16[896,512]{1,0:T(8,128)(2,1)}, bf16[896,512]{1,0:T(8,128)(2,1)S(1)}, u32[]{:S(2)}, u32[]{:S(2)}) collective-permute-start(bf16[896,512]{1,0:T(8,128)(2,1)} %get-tuple-element.76.refs_0_), channel_id=1, source_target_pairs={{0,8},{4,12},{8,16},{12,20},{16,24},{20,28},{1,9},{5,13},{9,17},{1... | collective-permute-start | bytes 2752520 | tf_op jit(solution)/shard_map/ppermute | solution.py:329
  109.4 8.1 %collective-permute-start.14 = (bf16[896,512]{1,0:T(8,128)(2,1)S(1)}, bf16[896,512]{1,0:T(8,128)(2,1)S(1)}, u32[]{:S(2)}, u32[]{:S(2)}) collective-permute-start(bf16[896,512]{1,0:T(8,128)(2,1)S(1)} %collective-permute-done.7.refs_8_), channel_id=1, source_target_pairs={{0,4},{4,0},{8,12},{12,8},{16,20},{20,16},{24,28},{28,24},{1,5},{5... | collective-permute-start | bytes 2752520 | tf_op jit(solution)/shard_map/ppermute | solution.py:336
  110.5 7.1 %collective-permute-start.15 = (bf16[896,512]{1,0:T(8,128)(2,1)S(1)}, bf16[896,512]{1,0:T(8,128)(2,1)S(1)}, u32[]{:S(2)}, u32[]{:S(2)}) collective-permute-start(bf16[896,512]{1,0:T(8,128)(2,1)S(1)} %collective-permute-done.8.refs_10_), channel_id=1, source_target_pairs={{0,4},{4,0},{8,12},{12,8},{16,20},{20,16},{24,28},{28,24},{1,5},{5... | collective-permute-start | bytes 2752520 | tf_op jit(solution)/shard_map/ppermute | solution.py:336
  110.5 26.9 %collective-permute-start.19 = (bf16[896,512]{1,0:T(8,128)(2,1)S(1)}, bf16[896,512]{1,0:T(8,128)(2,1)}, u32[]{:S(2)}, u32[]{:S(2)}) collective-permute-start(bf16[896,512]{1,0:T(8,128)(2,1)S(1)} %collective-permute-done.9.refs_0_), channel_id=1, source_target_pairs={{0,8},{4,12},{8,16},{12,20},{16,24},{20,28},{1,9},{5,13},{9,17},{1... | collective-permute-start | bytes 2752520 | tf_op jit(solution)/shard_map/ppermute | solution.py:329
  115.4 30.5 %collective-permute-start.23 = (bf16[896,512]{1,0:T(8,128)(2,1)S(1)}, bf16[896,512]{1,0:T(8,128)(2,1)S(1)}, u32[]{:S(2)}, u32[]{:S(2)}) collective-permute-start(bf16[896,512]{1,0:T(8,128)(2,1)S(1)} %collective-permute-done.9.refs_0_), channel_id=1, source_target_pairs={{0,4},{4,0},{8,12},{12,8},{16,20},{20,16},{24,28},{28,24},{1,5},{5... | collective-permute-start | bytes 2752520 | tf_op jit(solution)/shard_map/ppermute | solution.py:336
  116.2 24.0 %collective-permute-start.20 = (bf16[896,512]{1,0:T(8,128)(2,1)S(1)}, bf16[896,512]{1,0:T(8,128)(2,1)}, u32[]{:S(2)}, u32[]{:S(2)}) collective-permute-start(bf16[896,512]{1,0:T(8,128)(2,1)S(1)} %collective-permute-done.10.refs_2_), channel_id=1, source_target_pairs={{8,0},{12,4},{16,8},{20,12},{24,16},{28,20},{9,1},{13,5},{17,9},{2... | collective-permute-start | bytes 2752520 | tf_op jit(solution)/shard_map/ppermute | solution.py:329
  117.5 29.7 %collective-permute-start.24 = (bf16[896,512]{1,0:T(8,128)(2,1)S(1)}, bf16[896,512]{1,0:T(8,128)(2,1)}, u32[]{:S(2)}, u32[]{:S(2)}) collective-permute-start(bf16[896,512]{1,0:T(8,128)(2,1)S(1)} %collective-permute-done.10.refs_2_), channel_id=1, source_target_pairs={{0,4},{4,0},{8,12},{12,8},{16,20},{20,16},{24,28},{28,24},{1,5},{5... | collective-permute-start | bytes 2752520 | tf_op jit(solution)/shard_map/ppermute | solution.py:336
  140.2 9.3 %collective-permute-start.25 = (bf16[896,512]{1,0:T(8,128)(2,1)}, bf16[896,512]{1,0:T(8,128)(2,1)}, u32[]{:S(2)}, u32[]{:S(2)}) collective-permute-start(bf16[896,512]{1,0:T(8,128)(2,1)} %collective-permute-done.19.refs_4_), channel_id=1, source_target_pairs={{0,4},{4,0},{8,12},{12,8},{16,20},{20,16},{24,28},{28,24},{1,5},{5... | collective-permute-start | bytes 2752520 | tf_op jit(solution)/shard_map/ppermute | solution.py:336
  140.9 8.7 %collective-permute-start.26 = (bf16[896,512]{1,0:T(8,128)(2,1)}, bf16[896,512]{1,0:T(8,128)(2,1)}, u32[]{:S(2)}, u32[]{:S(2)}) collective-permute-start(bf16[896,512]{1,0:T(8,128)(2,1)} %collective-permute-done.20.refs_6_), channel_id=1, source_target_pairs={{0,4},{4,0},{8,12},{12,8},{16,20},{20,16},{24,28},{28,24},{1,5},{5... | collective-permute-start | bytes 2752520 | tf_op jit(solution)/shard_map/ppermute | solution.py:336
  143.6 39.1 %collective-permute-start.21 = (bf16[896,512]{1,0:T(8,128)(2,1)}, bf16[896,512]{1,0:T(8,128)(2,1)S(1)}, u32[]{:S(2)}, u32[]{:S(2)}) collective-permute-start(bf16[896,512]{1,0:T(8,128)(2,1)} %collective-permute-done.19.refs_4_), channel_id=1, source_target_pairs={{0,8},{4,12},{8,16},{12,20},{16,24},{20,28},{1,9},{5,13},{9,17},{1... | collective-permute-start | bytes 2752520 | tf_op jit(solution)/shard_map/ppermute | solution.py:329
  145.9 36.8 %collective-permute-start.22 = (bf16[896,512]{1,0:T(8,128)(2,1)}, bf16[896,512]{1,0:T(8,128)(2,1)S(1)}, u32[]{:S(2)}, u32[]{:S(2)}) collective-permute-start(bf16[896,512]{1,0:T(8,128)(2,1)} %collective-permute-done.20.refs_6_), channel_id=1, source_target_pairs={{8,0},{12,4},{16,8},{20,12},{24,16},{28,20},{9,1},{13,5},{17,9},{2... | collective-permute-start | bytes 2752520 | tf_op jit(solution)/shard_map/ppermute | solution.py:329
  147.2 35.5 %collective-permute-start.18 = (f16[912,512]{1,0:T(8,128)(2,1)}, f16[912,512]{1,0:T(8,128)(2,1)S(1)}, u32[]{:S(2)}, u32[]{:S(2)}) collective-permute-start(f16[912,512]{1,0:T(8,128)(2,1)} %pad_maximum_fusion.7), channel_id=1, source_target_pairs={{0,3},{1,0},{2,1},{3,2},{4,7},{5,4},{6,5},{7,6},{8,11},{9,8},{10,9... | collective-permute-start | bytes 2801672 | tf_op jit(solution)/shard_map/ppermute | solution.py:412
  149.5 33.3 %collective-permute-start.17 = (f16[912,512]{1,0:T(8,128)(2,1)}, f16[912,512]{1,0:T(8,128)(2,1)S(1)}, u32[]{:S(2)}, u32[]{:S(2)}) collective-permute-start(f16[912,512]{1,0:T(8,128)(2,1)} %pad_maximum_fusion.6), channel_id=1, source_target_pairs={{0,2},{1,3},{2,0},{3,1},{4,6},{5,7},{6,4},{7,5},{8,10},{9,11},{10,... | collective-permute-start | bytes 2801672 | tf_op jit(solution)/shard_map/ppermute | solution.py:412
  149.7 40.6 %collective-permute-start.16 = (f16[912,512]{1,0:T(8,128)(2,1)}, f16[912,512]{1,0:T(8,128)(2,1)S(1)}, u32[]{:S(2)}, u32[]{:S(2)}) collective-permute-start(f16[912,512]{1,0:T(8,128)(2,1)} %pad_maximum_fusion.5), channel_id=1, source_target_pairs={{0,1},{1,2},{2,3},{3,0},{4,5},{5,6},{6,7},{7,4},{8,9},{9,10},{10,1... | collective-permute-start | bytes 2801672 | tf_op jit(solution)/shard_map/ppermute | solution.py:412
  191.1 9.4 %collective-permute-start.28 = (bf16[896,512]{1,0:T(8,128)(2,1)S(1)}, bf16[896,512]{1,0:T(8,128)(2,1)S(1)}, u32[]{:S(2)}, u32[]{:S(2)}) collective-permute-start(bf16[896,512]{1,0:T(8,128)(2,1)S(1)} %collective-permute-done.21.refs_8_), channel_id=1, source_target_pairs={{0,4},{4,0},{8,12},{12,8},{16,20},{20,16},{24,28},{28,24},{1,5},{5... | collective-permute-start | bytes 2752520 | tf_op jit(solution)/shard_map/ppermute | solution.py:336
  193.7 6.8 %collective-permute-start.29 = (bf16[896,512]{1,0:T(8,128)(2,1)S(1)}, bf16[896,512]{1,0:T(8,128)(2,1)S(1)}, u32[]{:S(2)}, u32[]{:S(2)}) collective-permute-start(bf16[896,512]{1,0:T(8,128)(2,1)S(1)} %collective-permute-done.22.refs_10_), channel_id=1, source_target_pairs={{0,4},{4,0},{8,12},{12,8},{16,20},{20,16},{24,28},{28,24},{1,5},{5... | collective-permute-start | bytes 2752520 | tf_op jit(solution)/shard_map/ppermute | solution.py:336
  200.0 11.3 %collective-permute-start.27 = (f32[256,512]{1,0:T(8,128)S(1)}, f32[256,512]{1,0:T(8,128)S(1)}, u32[]{:S(2)}, u32[]{:S(2)}) collective-permute-start(f32[256,512]{1,0:T(8,128)S(1)} %constant_dynamic-slice_fusion.13), channel_id=1, source_target_pairs={{0,4},{4,0},{8,12},{12,8},{16,20},{20,16},{24,28},{28,24},{1,5},{5... | collective-permute-start | bytes 1572872 | tf_op jit(solution)/shard_map/ppermute | solution.py:452
  209.6 59.1 %collective-permute-start.34 = (f16[912,512]{1,0:T(8,128)(2,1)}, f16[912,512]{1,0:T(8,128)(2,1)}, u32[]{:S(2)}, u32[]{:S(2)}) collective-permute-start(f16[912,512]{1,0:T(8,128)(2,1)} %pad_maximum_fusion.9), channel_id=1, source_target_pairs={{0,2},{1,3},{2,0},{3,1},{4,6},{5,7},{6,4},{7,5},{8,10},{9,11},{10,... | collective-permute-start | bytes 2801672 | tf_op jit(solution)/shard_map/ppermute | solution.py:412
  211.0 57.7 %collective-permute-start.33 = (f16[912,512]{1,0:T(8,128)(2,1)}, f16[912,512]{1,0:T(8,128)(2,1)}, u32[]{:S(2)}, u32[]{:S(2)}) collective-permute-start(f16[912,512]{1,0:T(8,128)(2,1)} %pad_maximum_fusion.8), channel_id=1, source_target_pairs={{0,1},{1,2},{2,3},{3,0},{4,5},{5,6},{6,7},{7,4},{8,9},{9,10},{10,1... | collective-permute-start | bytes 2801672 | tf_op jit(solution)/shard_map/ppermute | solution.py:412
  220.5 48.2 %collective-permute-start.35 = (f16[912,512]{1,0:T(8,128)(2,1)S(1)}, f16[912,512]{1,0:T(8,128)(2,1)S(1)}, u32[]{:S(2)}, u32[]{:S(2)}) collective-permute-start(f16[912,512]{1,0:T(8,128)(2,1)S(1)} %pad_maximum_fusion.10), channel_id=1, source_target_pairs={{0,3},{1,0},{2,1},{3,2},{4,7},{5,4},{6,5},{7,6},{8,11},{9,8},{10,9... | collective-permute-start | bytes 2801672 | tf_op jit(solution)/shard_map/ppermute | solution.py:412
  222.7 34.2 %collective-permute-start.30 = (f32[64,512]{1,0:T(8,128)S(1)}, f32[64,512]{1,0:T(8,128)S(1)}, u32[]{:S(2)}, u32[]{:S(2)}) collective-permute-start(f32[64,512]{1,0:T(8,128)S(1)} %get-tuple-element.161), channel_id=1, source_target_pairs={{0,1},{1,2},{2,3},{3,0},{4,5},{5,6},{6,7},{7,4},{8,9},{9,10},{10,1... | collective-permute-start | bytes 393224 | tf_op jit(solution)/shard_map/ppermute | solution.py:452
  222.8 34.2 %collective-permute-start.31 = (f32[64,512]{1,0:T(8,128)S(1)}, f32[64,512]{1,0:T(8,128)S(1)}, u32[]{:S(2)}, u32[]{:S(2)}) collective-permute-start(f32[64,512]{1,0:T(8,128)S(1)} %get-tuple-element.160), channel_id=1, source_target_pairs={{0,2},{1,3},{2,0},{3,1},{4,6},{5,7},{6,4},{7,5},{8,10},{9,11},{10,... | collective-permute-start | bytes 393224 | tf_op jit(solution)/shard_map/ppermute | solution.py:452
  257.0 3.8 collective-permute-start.32
  260.9 4.6 %collective-permute-start.36 = (f32[16,512]{1,0:T(8,128)S(1)}, f32[16,512]{1,0:T(8,128)S(1)}, u32[]{:S(2)}, u32[]{:S(2)}) collective-permute-start(f32[16,512]{1,0:T(8,128)S(1)} %get-tuple-element.167), channel_id=1, source_target_pairs={{0,8},{4,12},{8,16},{12,20},{16,24},{20,28},{24,0},{28,4},{1,9},{5... | collective-permute-start | bytes 98312 | tf_op jit(solution)/shard_map/ppermute | solution.py:452
  264.0 3.8 collective-permute-start.37
  265.5 3.2 collective-permute-start.38
  282.0 11.1 %collective-permute-start.42 = (f32[512,512]{1,0:T(8,128)S(1)}, f32[512,512]{1,0:T(8,128)}, u32[]{:S(2)}, u32[]{:S(2)}) collective-permute-start(f32[512,512]{1,0:T(8,128)S(1)} %constant_dynamic-slice_fusion.6), channel_id=1, source_target_pairs={{0,4},{4,0},{8,12},{12,8},{16,20},{20,16},{24,28},{28,24},{1,5},{5... | collective-permute-start | bytes 3145736 | tf_op jit(solution)/shard_map/ppermute | solution.py:452
  286.5 4.6 %collective-permute-start.39 = (f32[16,512]{1,0:T(8,128)S(1)}, f32[16,512]{1,0:T(8,128)S(1)}, u32[]{:S(2)}, u32[]{:S(2)}) collective-permute-start(f32[16,512]{1,0:T(8,128)S(1)} %get-tuple-element.148), channel_id=1, source_target_pairs={{0,8},{4,12},{8,16},{12,20},{16,24},{20,28},{24,0},{28,4},{1,9},{5... | collective-permute-start | bytes 98312 | tf_op jit(solution)/shard_map/ppermute | solution.py:472
  287.8 5.2 %collective-permute-start.40 = (f32[16,512]{1,0:T(8,128)S(1)}, f32[16,512]{1,0:T(8,128)S(1)}, u32[]{:S(2)}, u32[]{:S(2)}) collective-permute-start(f32[16,512]{1,0:T(8,128)S(1)} %get-tuple-element.148), channel_id=1, source_target_pairs={{0,16},{4,20},{8,24},{12,28},{16,0},{20,4},{24,8},{28,12},{1,17},{... | collective-permute-start | bytes 98312 | tf_op jit(solution)/shard_map/ppermute | solution.py:472
  289.0 4.0 collective-permute-start.41
  294.9 20.4 %collective-permute-start.46 = (f32[128,512]{1,0:T(8,128)S(1)}, f32[128,512]{1,0:T(8,128)S(1)}, u32[]{:S(2)}, u32[]{:S(2)}) collective-permute-start(f32[128,512]{1,0:T(8,128)S(1)} %get-tuple-element.158), channel_id=1, source_target_pairs={{0,1},{1,2},{2,3},{3,0},{4,5},{5,6},{6,7},{7,4},{8,9},{9,10},{10,1... | collective-permute-start | bytes 786440 | tf_op jit(solution)/shard_map/ppermute | solution.py:452
  295.6 10.1 %collective-permute-start.43 = (f32[64,512]{1,0:T(8,128)S(1)}, f32[64,512]{1,0:T(8,128)S(1)}, u32[]{:S(2)}, u32[]{:S(2)}) collective-permute-start(f32[64,512]{1,0:T(8,128)S(1)} %constant_dynamic-update-slice_fusion.16), channel_id=1, source_target_pairs={{0,1},{1,2},{2,3},{3,0},{4,5},{5,6},{6,7},{7,4},{8,9},{9,10},{10,1... | collective-permute-start | bytes 393224 | tf_op jit(solution)/shard_map/ppermute | solution.py:472
  297.3 18.0 %collective-permute-start.47 = (f32[128,512]{1,0:T(8,128)S(1)}, f32[128,512]{1,0:T(8,128)S(1)}, u32[]{:S(2)}, u32[]{:S(2)}) collective-permute-start(f32[128,512]{1,0:T(8,128)S(1)} %get-tuple-element.157), channel_id=1, source_target_pairs={{0,2},{1,3},{2,0},{3,1},{4,6},{5,7},{6,4},{7,5},{8,10},{9,11},{10,... | collective-permute-start | bytes 786440 | tf_op jit(solution)/shard_map/ppermute | solution.py:452
  297.7 17.7 %collective-permute-start.48 = (f32[128,512]{1,0:T(8,128)S(1)}, f32[128,512]{1,0:T(8,128)S(1)}, u32[]{:S(2)}, u32[]{:S(2)}) collective-permute-start(f32[128,512]{1,0:T(8,128)S(1)} %get-tuple-element.156), channel_id=1, source_target_pairs={{0,3},{1,0},{2,1},{3,2},{4,7},{5,4},{6,5},{7,6},{8,11},{9,8},{10,9... | collective-permute-start | bytes 786440 | tf_op jit(solution)/shard_map/ppermute | solution.py:452
  298.6 16.7 %collective-permute-start.44 = (f32[64,512]{1,0:T(8,128)S(1)}, f32[64,512]{1,0:T(8,128)S(1)}, u32[]{:S(2)}, u32[]{:S(2)}) collective-permute-start(f32[64,512]{1,0:T(8,128)S(1)} %constant_dynamic-update-slice_fusion.16), channel_id=1, source_target_pairs={{0,2},{1,3},{2,0},{3,1},{4,6},{5,7},{6,4},{7,5},{8,10},{9,11},{10,... | collective-permute-start | bytes 393224 | tf_op jit(solution)/shard_map/ppermute | solution.py:472
  305.7 9.6 %collective-permute-start.45 = (f32[64,512]{1,0:T(8,128)S(1)}, f32[64,512]{1,0:T(8,128)S(1)}, u32[]{:S(2)}, u32[]{:S(2)}) collective-permute-start(f32[64,512]{1,0:T(8,128)S(1)} %constant_dynamic-update-slice_fusion.16), channel_id=1, source_target_pairs={{0,3},{1,0},{2,1},{3,2},{4,7},{5,4},{6,5},{7,6},{8,11},{9,8},{10,9... | collective-permute-start | bytes 393224 | tf_op jit(solution)/shard_map/ppermute | solution.py:472
  316.2 9.4 %collective-permute-start.49 = (f32[256,512]{1,0:T(8,128)S(1)}, f32[256,512]{1,0:T(8,128)}, u32[]{:S(2)}, u32[]{:S(2)}) collective-permute-start(f32[256,512]{1,0:T(8,128)S(1)} %constant_dynamic-update-slice_fusion.12), channel_id=1, source_target_pairs={{0,4},{4,0},{8,12},{12,8},{16,20},{20,16},{24,28},{28,24},{1,5},{5... | collective-permute-start | bytes 1572872 | tf_op jit(solution)/shard_map/ppermute | solution.py:472
  317.9 5.6 %collective-permute-start.50 = (f32[32,512]{1,0:T(8,128)S(1)}, f32[32,512]{1,0:T(8,128)S(1)}, u32[]{:S(2)}, u32[]{:S(2)}) collective-permute-start(f32[32,512]{1,0:T(8,128)S(1)} %get-tuple-element.164), channel_id=1, source_target_pairs={{0,8},{4,12},{8,16},{12,20},{16,24},{20,28},{24,0},{28,4},{1,9},{5... | collective-permute-start | bytes 196616 | tf_op jit(solution)/shard_map/ppermute | solution.py:452
  318.4 7.2 %collective-permute-start.51 = (f32[32,512]{1,0:T(8,128)S(1)}, f32[32,512]{1,0:T(8,128)S(1)}, u32[]{:S(2)}, u32[]{:S(2)}) collective-permute-start(f32[32,512]{1,0:T(8,128)S(1)} %get-tuple-element.163), channel_id=1, source_target_pairs={{0,16},{4,20},{8,24},{12,28},{16,0},{20,4},{24,8},{28,12},{1,17},{... | collective-permute-start | bytes 196616 | tf_op jit(solution)/shard_map/ppermute | solution.py:452
  319.9 5.7 %collective-permute-start.52 = (f32[32,512]{1,0:T(8,128)S(1)}, f32[32,512]{1,0:T(8,128)S(1)}, u32[]{:S(2)}, u32[]{:S(2)}) collective-permute-start(f32[32,512]{1,0:T(8,128)S(1)} %get-tuple-element.162), channel_id=1, source_target_pairs={{0,24},{4,28},{8,0},{12,4},{16,8},{20,12},{24,16},{28,20},{1,25},{... | collective-permute-start | bytes 196616 | tf_op jit(solution)/shard_map/ppermute | solution.py:452
  326.8 31.6 %collective-permute-start.53 = (f32[32,512]{1,0:T(8,128)S(1)}, f32[32,512]{1,0:T(8,128)S(1)}, u32[]{:S(2)}, u32[]{:S(2)}) collective-permute-start(f32[32,512]{1,0:T(8,128)S(1)} %get-tuple-element.146), channel_id=1, source_target_pairs={{0,8},{4,12},{8,16},{12,20},{16,24},{20,28},{24,0},{28,4},{1,9},{5... | collective-permute-start | bytes 196616 | tf_op jit(solution)/shard_map/ppermute | solution.py:472
  328.6 29.7 %collective-permute-start.54 = (f32[32,512]{1,0:T(8,128)S(1)}, f32[32,512]{1,0:T(8,128)S(1)}, u32[]{:S(2)}, u32[]{:S(2)}) collective-permute-start(f32[32,512]{1,0:T(8,128)S(1)} %get-tuple-element.146), channel_id=1, source_target_pairs={{0,16},{4,20},{8,24},{12,28},{16,0},{20,4},{24,8},{28,12},{1,17},{... | collective-permute-start | bytes 196616 | tf_op jit(solution)/shard_map/ppermute | solution.py:472
  330.0 28.3 %collective-permute-start.55 = (f32[32,512]{1,0:T(8,128)S(1)}, f32[32,512]{1,0:T(8,128)S(1)}, u32[]{:S(2)}, u32[]{:S(2)}) collective-permute-start(f32[32,512]{1,0:T(8,128)S(1)} %get-tuple-element.146), channel_id=1, source_target_pairs={{0,24},{4,28},{8,0},{12,4},{16,8},{20,12},{24,16},{28,20},{1,25},{... | collective-permute-start | bytes 196616 | tf_op jit(solution)/shard_map/ppermute | solution.py:472
  358.4 7.3 %collective-permute-start.56 = (f32[128,512]{1,0:T(8,128)S(1)}, f32[128,512]{1,0:T(8,128)S(1)}, u32[]{:S(2)}, u32[]{:S(2)}) collective-permute-start(f32[128,512]{1,0:T(8,128)S(1)} %constant_dynamic-update-slice_fusion.6), channel_id=1, source_target_pairs={{0,1},{1,2},{2,3},{3,0},{4,5},{5,6},{6,7},{7,4},{8,9},{9,10},{10,1... | collective-permute-start | bytes 786440 | tf_op jit(solution)/shard_map/ppermute | solution.py:472
  360.0 13.2 %collective-permute-start.57 = (f32[128,512]{1,0:T(8,128)S(1)}, f32[128,512]{1,0:T(8,128)S(1)}, u32[]{:S(2)}, u32[]{:S(2)}) collective-permute-start(f32[128,512]{1,0:T(8,128)S(1)} %constant_dynamic-update-slice_fusion.6), channel_id=1, source_target_pairs={{0,2},{1,3},{2,0},{3,1},{4,6},{5,7},{6,4},{7,5},{8,10},{9,11},{10,... | collective-permute-start | bytes 786440 | tf_op jit(solution)/shard_map/ppermute | solution.py:472
  360.9 12.3 %collective-permute-start.58 = (f32[128,512]{1,0:T(8,128)S(1)}, f32[128,512]{1,0:T(8,128)S(1)}, u32[]{:S(2)}, u32[]{:S(2)}) collective-permute-start(f32[128,512]{1,0:T(8,128)S(1)} %constant_dynamic-update-slice_fusion.6), channel_id=1, source_target_pairs={{0,3},{1,0},{2,1},{3,2},{4,7},{5,4},{6,5},{7,6},{8,11},{9,8},{10,9... | collective-permute-start | bytes 786440 | tf_op jit(solution)/shard_map/ppermute | solution.py:472
  373.3 2.8 collective-permute-start.59
  (31 other events, 226.3 us)
where the time goes:
time: 439 us; the launch traced here: 430 us
  Pallas kernels  171 us (39%)
  waiting for transfers between devices  91.3 us (21%)
  starting transfers between devices  77 us (18%)
  local copies, waits for them, and re-layouts  48.7 us (11%)
  other arithmetic  24.5 us (6%)
  matrix products  15.6 us (4%)
    pallas_call x9, Pallas kernels, level_product(): pl.pallas_call(functools.partial(level_kernel, pieces, len(blocks) // 2,...  106 us
    pallas_call x4, Pallas kernels, factor_column(): pl.pallas_call(functools.partial(column_kernel, scale, before, width), ou...  64.9 us
    ppermute x14, waiting for transfers between devices, task(): put(('add', c, step), lax.ppermute(piece, axis, perm(step)), line.now + 1)  44.6 us
    unnamed x71, local copies, waits for them, and re-layouts  33.2 us
    ppermute x12, starting transfers between devices, task(): put((way, c, step), lax.ppermute(source, 'row', perm), arrival[c, step])  31.9 us
    ppermute x14, waiting for transfers between devices, task(): lax.ppermute(get(('sum', c)), axis, perm(step))  30.1 us
    ppermute x14, starting transfers between devices, task(): put(('add', c, step), lax.ppermute(piece, axis, perm(step)), line.now + 1)  15.6 us
    ppermute x14, starting transfers between devices, task(): lax.ppermute(get(('sum', c)), axis, perm(step))  15.1 us
  transfers between devices with their start and end apart: 60, of which 19 were waited for; matrix products, arithmetic and copies ran while one was open for 7% of the time, Pallas kernels for 31%

commit v1 on v0

--- a/solution.py
+++ b/solution.py
@@ -103,7 +103,7 @@
             ],
         ),
         input_output_aliases={2 + len(blocks): 0} if whole else {},
-        compiler_params=pltpu.CompilerParams(vmem_limit_bytes=24 * 1024 * 1024),
+        compiler_params=pltpu.CompilerParams(vmem_limit_bytes=14 * 1024 * 1024),
         cost_estimate=pl.CostEstimate(
             flops=2 * pieces * rows * depth * width, bytes_accessed=2 * pieces * rows * depth, transcendentals=0
         ),
@@ -300,6 +300,46 @@
     )(*operands)
 
 
+def halves(x):
+    high = x.astype(jnp.bfloat16)
+    return high, (x - high.astype(jnp.float32)).astype(jnp.bfloat16)
+
+
+def basis_kernel(x_ref, rows_ref, *refs):
+    out_ref = refs[-1]
+    x_high, x_low = halves(x_ref[...])
+    w_high, w_low = halves(rows_ref[...])
+
+    def nt(a, b):
+        return lax.dot_general(a, b, (((1,), (1,)), ((), ())), preferred_element_type=jnp.float32)
+
+    value = nt(x_high, w_high) + (nt(x_high, w_low) + nt(x_low, w_high))
+    done = out_ref.shape[1] - value.shape[1]
+    if done:
+        out_ref[:, :done] = refs[0][...]
+    out_ref[:, done:] = value
+
+
+def basis_product(x, last_rows, before):
+    rows, depth = x.shape
+    tile = rows // 2 if rows % 32 == 0 else rows
+    operands = (x, last_rows) if before is None else (x, last_rows, before)
+    specs = [pl.BlockSpec((tile, depth), lambda i: (i, 0)), pl.BlockSpec(last_rows.shape, lambda i: (0, 0))]
+    if before is not None:
+        specs.append(pl.BlockSpec((tile, before.shape[1]), lambda i: (i, 0)))
+    return pl.pallas_call(
+        basis_kernel,
+        out_shape=jax.ShapeDtypeStruct((rows, depth), jnp.float32),
+        grid=(rows // tile,),
+        in_specs=specs,
+        out_specs=pl.BlockSpec((tile, depth), lambda i: (i, 0)),
+        compiler_params=pltpu.CompilerParams(vmem_limit_bytes=32 * 1024 * 1024),
+        cost_estimate=pl.CostEstimate(
+            flops=6 * rows * depth * last_rows.shape[0], bytes_accessed=8 * rows * depth, transcendentals=0
+        ),
+    )(*operands)
+
+
 def body(row_size, col_size, factor, subspace):
     rows = subspace.shape[0]
     total_rows = rows * row_size * col_size
@@ -436,7 +476,7 @@
                 get(("so far", c)),
                 get(("image", c)),
                 (((0,), (0,)), ((), ())),
-                precision=HIGHEST,
+                precision=lax.Precision.HIGH,
                 preferred_element_type=jnp.float32,
             )
 
@@ -507,13 +547,8 @@
 
     def multiply_basis(c):
         def task():
-            line.values["basis", c] = lax.dot_general(
-                get(("so far", c)),
-                get(("last", c)),
-                (((1,), (1,)), ((), ())),
-                precision=lax.Precision.HIGH,
-                preferred_element_type=jnp.float32,
-            )
+            before = get(("basis", c - 1)) if c else None
+            line.values["basis", c] = basis_product(get(("so far", c)), get(("last", c)), before)
 
         return task
 
@@ -555,7 +590,7 @@
             line.advance()
         for task in tasks.get(slot, []):
             task()
-    basis = jnp.concatenate([get(("basis", c)) for c in range(chunks)], axis=1)
+    basis = get(("basis", chunks - 1))
     upper = jnp.concatenate(
         [get(("column", end)) for end in range(COLUMN, subspace.shape[1] + 1, COLUMN)], axis=1
     )

time: 439 us -> 429 us (0.977)
  matrix products: 15.6 us -> 5.31 us
  local copies, waits for them, and re-layouts: 48.7 us -> 42.2 us
  Pallas kernels: 171 us -> 177 us
    unnamed x71 -> x74, local copies, waits for them, and re-layouts: 33.2 us -> 26.1 us
    pallas_call x0 -> x2, Pallas kernels: none -> 6.4 us  [basis_product(): pl.pallas_call(basis_kernel, out_shape=jax.ShapeDtypeStruct((rows, depth)...]
    dot_general x2 -> x0, matrix products: 5.4 us -> none  [task(): lax.dot_general(get(('so far', c)), get(('last', c)), (((1,), (1,)), ((),...]
    dot_general x2, matrix products: 10.2 us -> 5.31 us  [task(): lax.dot_general(get(('so far', c)), get(('image', c)), (((0,), (0,)), (()...]
  transfers between devices with their start and end apart: 60 -> 60, of which waited for: 19 -> 18; matrix products, arithmetic and copies ran while one was open for 7% -> 7% of each run, Pallas kernels for 31% -> 32%
where the time goes in v1:
time: 429 us; the launch traced here: 421 us
  Pallas kernels  177 us (41%)
  waiting for transfers between devices  91.1 us (21%)
  starting transfers between devices  77.1 us (18%)
  local copies, waits for them, and re-layouts  42.2 us (10%)
  other arithmetic  25.7 us (6%)
  matrix products  5.31 us (1%)
    pallas_call x9, Pallas kernels, level_product(): pl.pallas_call(functools.partial(level_kernel, pieces, len(blocks) // 2,...  106 us
    pallas_call x4, Pallas kernels, factor_column(): pl.pallas_call(functools.partial(column_kernel, scale, before, width), ou...  65 us
    ppermute x14, waiting for transfers between devices, task(): put(('add', c, step), lax.ppermute(piece, axis, perm(step)), line.now + 1)  44.4 us
    ppermute x12, starting transfers between devices, task(): put((way, c, step), lax.ppermute(source, 'row', perm), arrival[c, step])  31.9 us
    ppermute x14, waiting for transfers between devices, task(): lax.ppermute(get(('sum', c)), axis, perm(step))  29.7 us
    unnamed x74, local copies, waits for them, and re-layouts  26.1 us
    ppermute x14, starting transfers between devices, task(): put(('add', c, step), lax.ppermute(piece, axis, perm(step)), line.now + 1)  16.2 us
    ppermute x14, starting transfers between devices, task(): lax.ppermute(get(('sum', c)), axis, perm(step))  15.1 us
  transfers between devices with their start and end apart: 60, of which 18 were waited for; matrix products, arithmetic and copies ran while one was open for 7% of the time, Pallas kernels for 32%

profile of v1, /device:TPU:1, one launch (start us, length us, event | category | flops | bytes accessed | tf_op | source)
XLA Modules:
  0.0 420.9 jit_solution(10624789857487500540)
XLA Ops:
  0.7 2.5 fusion.29
  3.2 4.7 %collective-permute-start = (bf16[896,512]{1,0:T(8,128)(2,1)S(1)}, bf16[896,512]{1,0:T(8,128)(2,1)S(1)}, u32[]{:S(2)}, u32[]{:S(2)}) collective-permute-start(bf16[896,512]{1,0:T(8,128)(2,1)S(1)} %get-tuple-element.152.refs_0_), channel_id=1, source_target_pairs={{0,8},{4,12},{8,16},{12,20},{16,24},{20,28},{1,9},{5,13},{9,17},{1... | collective-permute-start | bytes 2752520 | tf_op jit(solution)/shard_map/ppermute | solution.py:369
  11.8 13.0 %shard_map.167.refs_4_ = f32[4,896,512]{2,1,0:T(8,128)S(1)} custom-call(s32[7]{0:T(128)S(1)} %stack.36.place_ref, bf16[3584,7168]{1,0:T(8,128)(2,1)} %factor_ref.17, bf16[896,512]{1,0:T(8,128)(2,1)S(1)} %get-tuple-element.152.refs_0_, bf16[896,512]{1,0:T(8,128)(2,1)} %collective-permute-done.2.refs_1_), custom_call_target="tpu_custom_call" | custom-call | flops 6576668672 | bytes 12845056 | tf_op jit(solution)/shard_map/pallas_call | solution.py:90
  24.9 3.0 copy-done
  27.8 3.6 collective-permute-done.1.refs_2_
  32.6 4.1 collective-permute-start.3
  39.3 1.4 stack.34.place_ref
  40.7 3.4 copy-done.1
  44.1 13.1 %shard_map.168.refs_8_ = f32[4,896,512]{2,1,0:T(8,128)S(1)} custom-call(s32[7]{0:T(128)S(1)} %stack.37.place_ref, bf16[3584,7168]{1,0:T(8,128)(2,1)} %factor_ref.17, bf16[896,512]{1,0:T(8,128)(2,1)S(1)} %collective-permute-done.refs_0_, bf16[896,512]{1,0:T(8,128)(2,1)S(1)} %collective-permute-done.5.refs_1_, ...), custom_call_target="tpu_custom_call", output_to_operand_aliasing={{}: (6, {})} | custom-call | flops 6576668672 | bytes 12845056 | tf_op jit(solution)/shard_map/pallas_call | solution.py:90
  57.2 2.9 copy-done.2
  64.5 1.4 collective-permute-start.10
  65.9 4.0 collective-permute-start.7
  72.2 4.0 collective-permute-start.9
  76.3 14.1 %shard_map.170.refs_4_ = f32[4,896,512]{2,1,0:T(8,128)S(1)} custom-call(s32[7]{0:T(128)S(1)} %stack.36.place_ref, bf16[3584,7168]{1,0:T(8,128)(2,1)} %factor_ref.17, bf16[896,512]{1,0:T(8,128)(2,1)} %get-tuple-element.76.refs_0_, bf16[896,512]{1,0:T(8,128)(2,1)} %collective-permute-done.13.refs_1_), custom_call_target="tpu_custom_call" | custom-call | flops 6576668672 | bytes 12845056 | tf_op jit(solution)/shard_map/pallas_call | solution.py:90
  90.4 3.0 copy-done.5
  93.4 13.2 %shard_map.169.refs_12_ = f32[4,896,512]{2,1,0:T(8,128)S(1)} custom-call(s32[7]{0:T(128)S(1)} %stack.34.place_ref, bf16[3584,7168]{1,0:T(8,128)(2,1)} %factor_ref.17, bf16[896,512]{1,0:T(8,128)(2,1)S(1)} %collective-permute-done.refs_0_, bf16[896,512]{1,0:T(8,128)(2,1)S(1)} %copy-done.19, ...), custom_call_target="tpu_custom_call", output_to_operand_aliasing={{}: (10, {})} | custom-call | flops 6576668672 | bytes 12845056 | tf_op jit(solution)/shard_map/pallas_call | solution.py:90
  106.6 1.7 collective-permute-done.8.refs_10_
  110.4 4.9 %collective-permute-start.19 = (bf16[896,512]{1,0:T(8,128)(2,1)S(1)}, bf16[896,512]{1,0:T(8,128)(2,1)}, u32[]{:S(2)}, u32[]{:S(2)}) collective-permute-start(bf16[896,512]{1,0:T(8,128)(2,1)S(1)} %collective-permute-done.9.refs_0_), channel_id=1, source_target_pairs={{0,8},{4,12},{8,16},{12,20},{16,24},{20,28},{1,9},{5,13},{9,17},{1... | collective-permute-start | bytes 2752520 | tf_op jit(solution)/shard_map/ppermute | solution.py:369
  118.7 12.1 %shard_map.171 = f32[4,896,512]{2,1,0:T(8,128)S(1)} custom-call(s32[7]{0:T(128)S(1)} %stack.33.place_ref, bf16[3584,7168]{1,0:T(8,128)(2,1)} %factor_ref.17, bf16[896,512]{1,0:T(8,128)(2,1)S(1)} %copy-done.15, bf16[896,512]{1,0:T(8,128)(2,1)S(1)} %copy-done.19, bf16[896,512]{1,0:T(8,128)(2,1)S(1)} %copy-done.17, ...), custom_call_target="tpu_custom_call", output_to_operand_aliasing={{}: (14, {})} | custom-call | flops 6576668672 | bytes 12845056 | tf_op jit(solution)/shard_map/pallas_call | solution.py:90
  132.3 1.5 copy-done.4
  137.3 2.8 collective-permute-done.20.refs_6_
  142.2 1.3 stack.41.place_ref
  143.5 2.2 collective-permute-start.21
  147.1 2.2 collective-permute-start.18
  150.1 3.1 copy-done.6
  153.2 13.1 %shard_map.172.refs_8_ = f32[4,896,512]{2,1,0:T(8,128)S(1)} custom-call(s32[7]{0:T(128)S(1)} %stack.37.place_ref, bf16[3584,7168]{1,0:T(8,128)(2,1)} %factor_ref.17, bf16[896,512]{1,0:T(8,128)(2,1)S(1)} %collective-permute-done.9.refs_0_, bf16[896,512]{1,0:T(8,128)(2,1)S(1)} %collective-permute-done.23.refs_1_, ...), custom_call_target="tpu_custom_call", output_to_operand_aliasing={{}: (6, {})} | custom-call | flops 6576668672 | bytes 12845056 | tf_op jit(solution)/shard_map/pallas_call | solution.py:90
  166.3 13.2 %shard_map.173.refs_12_ = f32[4,896,512]{2,1,0:T(8,128)S(1)} custom-call(s32[7]{0:T(128)S(1)} %stack.34.place_ref, bf16[3584,7168]{1,0:T(8,128)(2,1)} %factor_ref.17, bf16[896,512]{1,0:T(8,128)(2,1)S(1)} %collective-permute-done.9.refs_0_, bf16[896,512]{1,0:T(8,128)(2,1)S(1)} %collective-permute-done.23.refs_1_, ...), custom_call_target="tpu_custom_call", output_to_operand_aliasing={{}: (10, {})} | custom-call | flops 6576668672 | bytes 12845056 | tf_op jit(solution)/shard_map/pallas_call | solution.py:90
  179.5 3.0 copy-done.7
  182.5 7.7 %collective-permute-done.16 = f16[912,512]{1,0:T(8,128)(2,1)S(1)} collective-permute-done((f16[912,512]{1,0:T(8,128)(2,1)}, f16[912,512]{1,0:T(8,128)(2,1)S(1)}, u32[]{:S(2)}, u32[]{:S(2)}) %collective-permute-start.16) | collective-permute-done | bytes 933920 | tf_op jit(solution)/shard_map/ppermute | solution.py:452
  191.0 2.6 collective-permute-start.28
  193.7 2.6 fusion.6.x_ref
  196.3 1.8 fusion.30
  198.7 7.1 %shard_map.174 = f32[2,896,512]{2,1,0:T(8,128)S(1)} custom-call(s32[5]{0:T(128)S(1)} %stack.38.place_ref, bf16[3584,7168]{1,0:T(8,128)(2,1)} %factor_ref.17, bf16[896,512]{1,0:T(8,128)(2,1)S(1)} %copy-done.11, bf16[896,512]{1,0:T(8,128)(2,1)S(1)} %copy-done.13, bf16[896,512]{1,0:T(8,128)(2,1)S(1)} %collective-permute-done.10.refs_2_, ...), custom_call_target="tpu_custom_call" | custom-call | flops 3288334336 | bytes 6422528 | tf_op jit(solution)/shard_map/pallas_call | solution.py:90
  209.6 7.1 %shard_map.175 = f32[2,896,512]{2,1,0:T(8,128)S(1)} custom-call(s32[5]{0:T(128)S(1)} %stack.41.place_ref, bf16[3584,7168]{1,0:T(8,128)(2,1)} %factor_ref.17, bf16[896,512]{1,0:T(8,128)(2,1)S(1)} %copy-done.11, bf16[896,512]{1,0:T(8,128)(2,1)S(1)} %copy-done.13, bf16[896,512]{1,0:T(8,128)(2,1)S(1)} %collective-permute-done.10.refs_2_, ...), custom_call_target="tpu_custom_call" | custom-call | flops 3288334336 | bytes 6422528 | tf_op jit(solution)/shard_map/pallas_call | solution.py:90
  217.1 1.4 copy-done.8
  218.7 2.1 collective-permute-start.32
  222.9 32.4 %collective-permute-done.33 = f32[64,512]{1,0:T(8,128)S(1)} collective-permute-done((f32[64,512]{1,0:T(8,128)S(1)}, f32[64,512]{1,0:T(8,128)S(1)}, u32[]{:S(2)}, u32[]{:S(2)}) %collective-permute-start.33) | collective-permute-done | bytes 131104 | tf_op jit(solution)/shard_map/ppermute | solution.py:492
  255.3 3.9 collective-permute-done.35
  260.8 3.2 collective-permute-start.36
  264.0 1.4 collective-permute-done.36
  268.6 1.4 convert_element_type.87
  270.1 1.6 convert_element_type.88
  271.7 1.4 convert_element_type.89
  274.1 3.5 fusion.9
  278.9 4.6 %collective-permute-start.42 = (f32[512,512]{1,0:T(8,128)S(1)}, f32[512,512]{1,0:T(8,128)}, u32[]{:S(2)}, u32[]{:S(2)}) collective-permute-start(f32[512,512]{1,0:T(8,128)S(1)} %constant_dynamic-slice_fusion.6), channel_id=1, source_target_pairs={{0,4},{4,0},{8,12},{12,8},{16,20},{20,16},{24,28},{28,24},{1,5},{5... | collective-permute-start | bytes 3145736 | tf_op jit(solution)/shard_map/ppermute | solution.py:492
  284.3 1.6 collective-permute-start.39
  289.0 2.0 collective-permute-done.40
  291.0 1.8 dynamic-slice_add_fusion
  293.6 1.8 collective-permute-start.43
  297.5 6.2 %collective-permute-done.43 = f32[64,512]{1,0:T(8,128)S(1)} collective-permute-done((f32[64,512]{1,0:T(8,128)S(1)}, f32[64,512]{1,0:T(8,128)S(1)}, u32[]{:S(2)}, u32[]{:S(2)}) %collective-permute-start.43) | collective-permute-done | bytes 131104 | tf_op jit(solution)/shard_map/ppermute | solution.py:512
  303.7 9.5 %collective-permute-done.44 = f32[64,512]{1,0:T(8,128)S(1)} collective-permute-done((f32[64,512]{1,0:T(8,128)S(1)}, f32[64,512]{1,0:T(8,128)S(1)}, u32[]{:S(2)}, u32[]{:S(2)}) %collective-permute-start.44) | collective-permute-done | bytes 131104 | tf_op jit(solution)/shard_map/ppermute | solution.py:512
  319.4 2.1 collective-permute-done.50
  321.5 2.7 collective-permute-done.51
  325.4 1.7 collective-permute-start.53
  329.5 12.4 %shard_map.176 = (f32[256,256]{1,0:T(8,128)S(1)}, f32[256,256]{1,0:T(8,128)S(1)}) custom-call(f32[256,256]{1,0:T(8,128)S(1)} %slice.128.gram_ref), custom_call_target="tpu_custom_call" | custom-call | flops 16000000000 | bytes 4000000 | tf_op jit(solution)/shard_map/pallas_call | solution.py:290
  341.9 14.8 %shard_map.177 = (f32[512,256]{1,0:T(8,128)S(1)}, f32[256,512]{1,0:T(8,128)S(1)}) custom-call(f32[512,256]{1,0:T(8,128)S(1)} %slice.129.gram_ref, f32[256,256]{1,0:T(8,128)S(1)} %get-tuple-element.120.refs_0_), custom_call_target="tpu_custom_call" | custom-call | flops 16000000000 | bytes 4000000 | tf_op jit(solution)/shard_map/pallas_call | solution.py:290
  357.0 1.6 collective-permute-start.56
  360.7 3.8 collective-permute-done.56
  364.5 7.2 %collective-permute-done.57 = f32[128,512]{1,0:T(8,128)S(1)} collective-permute-done((f32[128,512]{1,0:T(8,128)S(1)}, f32[128,512]{1,0:T(8,128)S(1)}, u32[]{:S(2)}, u32[]{:S(2)}) %collective-permute-start.57) | collective-permute-done | bytes 262176 | tf_op jit(solution)/shard_map/ppermute | solution.py:512
  372.8 1.9 shard_map.180.refs_0_
  375.3 16.3 %shard_map.178 = (f32[768,256]{1,0:T(8,128)S(1)}, f32[256,768]{1,0:T(8,128)S(1)}) custom-call(f32[768,256]{1,0:T(8,128)S(1)} %slice.130.gram_ref, f32[512,512]{1,0:T(8,128)S(1)} %select_maximum_fusion.3.refs_0_.rows_ref), custom_call_target="tpu_custom_call" | custom-call | flops 16000000000 | bytes 4000000 | tf_op jit(solution)/shard_map/pallas_call | solution.py:290
  391.8 21.4 %shard_map.179 = (f32[1024,256]{1,0:T(8,128)S(1)}, f32[256,1024]{1,0:T(8,128)S(1)}) custom-call(f32[1024,256]{1,0:T(8,128)S(1)} %slice.131.gram_ref, f32[768,768]{1,0:T(8,128)S(1)} %select_maximum_fusion.2.refs_0_), custom_call_target="tpu_custom_call" | custom-call | flops 16000000000 | bytes 4000000 | tf_op jit(solution)/shard_map/pallas_call | solution.py:290
  413.5 4.5 %shard_map.181 = f32[896,1024]{1,0:T(8,128)} custom-call(f32[896,1024]{1,0:T(8,128)S(1)} %pad_maximum_fusion.x_ref, f32[512,1024]{1,0:T(8,128)S(1)} %pad_maximum_fusion.1.rows_ref, f32[896,512]{1,0:T(8,128)S(1)} %shard_map.180.refs_0_), custom_call_target="tpu_custom_call" | custom-call | flops 2818572288 | bytes 7340032 | tf_op jit(solution)/shard_map/pallas_call | solution.py:330
  418.1 2.6 fusion
  (243 shorter events, 64.3 us)
Async XLA Ops:
  3.2 8.7 %collective-permute-start.2 = (bf16[896,512]{1,0:T(8,128)(2,1)S(1)}, bf16[896,512]{1,0:T(8,128)(2,1)}, u32[]{:S(2)}, u32[]{:S(2)}) collective-permute-start(bf16[896,512]{1,0:T(8,128)(2,1)S(1)} %get-tuple-element.152.refs_0_), channel_id=1, source_target_pairs={{0,4},{4,0},{8,12},{12,8},{16,20},{20,16},{24,28},{28,24},{1,5},{5... | collective-permute-start | bytes 2752520 | tf_op jit(solution)/shard_map/ppermute | solution.py:376
  3.2 24.6 %collective-permute-start = (bf16[896,512]{1,0:T(8,128)(2,1)S(1)}, bf16[896,512]{1,0:T(8,128)(2,1)S(1)}, u32[]{:S(2)}, u32[]{:S(2)}) collective-permute-start(bf16[896,512]{1,0:T(8,128)(2,1)S(1)} %get-tuple-element.152.refs_0_), channel_id=1, source_target_pairs={{0,8},{4,12},{8,16},{12,20},{16,24},{20,28},{1,9},{5,13},{9,17},{1... | collective-permute-start | bytes 2752520 | tf_op jit(solution)/shard_map/ppermute | solution.py:369
  7.9 23.6 %collective-permute-start.1 = (bf16[896,512]{1,0:T(8,128)(2,1)S(1)}, bf16[896,512]{1,0:T(8,128)(2,1)S(1)}, u32[]{:S(2)}, u32[]{:S(2)}) collective-permute-start(bf16[896,512]{1,0:T(8,128)(2,1)S(1)} %get-tuple-element.152.refs_0_), channel_id=1, source_target_pairs={{8,0},{12,4},{16,8},{20,12},{24,16},{28,20},{9,1},{13,5},{17,9},{2... | collective-permute-start | bytes 2752520 | tf_op jit(solution)/shard_map/ppermute | solution.py:369
  27.8 65.5 %copy-start.14 = (bf16[896,512]{1,0:T(8,128)(2,1)}, bf16[896,512]{1,0:T(8,128)(2,1)S(1)}, u32[]{:S(2)}) copy-start(bf16[896,512]{1,0:T(8,128)(2,1)S(1)} %collective-permute-done.refs_0_) | copy-start | bytes 2752516
  31.5 9.2 %collective-permute-start.5 = (bf16[896,512]{1,0:T(8,128)(2,1)S(1)}, bf16[896,512]{1,0:T(8,128)(2,1)S(1)}, u32[]{:S(2)}, u32[]{:S(2)}) collective-permute-start(bf16[896,512]{1,0:T(8,128)(2,1)S(1)} %collective-permute-done.refs_0_), channel_id=1, source_target_pairs={{0,4},{4,0},{8,12},{12,8},{16,20},{20,16},{24,28},{28,24},{1,5},{5... | collective-permute-start | bytes 2752520 | tf_op jit(solution)/shard_map/ppermute | solution.py:376
  32.6 8.1 %collective-permute-start.6 = (bf16[896,512]{1,0:T(8,128)(2,1)S(1)}, bf16[896,512]{1,0:T(8,128)(2,1)}, u32[]{:S(2)}, u32[]{:S(2)}) collective-permute-start(bf16[896,512]{1,0:T(8,128)(2,1)S(1)} %collective-permute-done.1.refs_2_), channel_id=1, source_target_pairs={{0,4},{4,0},{8,12},{12,8},{16,20},{20,16},{24,28},{28,24},{1,5},{5... | collective-permute-start | bytes 2752520 | tf_op jit(solution)/shard_map/ppermute | solution.py:376
  32.6 27.5 %collective-permute-start.3 = (bf16[896,512]{1,0:T(8,128)(2,1)S(1)}, bf16[896,512]{1,0:T(8,128)(2,1)}, u32[]{:S(2)}, u32[]{:S(2)}) collective-permute-start(bf16[896,512]{1,0:T(8,128)(2,1)S(1)} %collective-permute-done.refs_0_), channel_id=1, source_target_pairs={{0,8},{4,12},{8,16},{12,20},{16,24},{20,28},{1,9},{5,13},{9,17},{1... | collective-permute-start | bytes 2752520 | tf_op jit(solution)/shard_map/ppermute | solution.py:369
  36.7 23.5 %collective-permute-start.4 = (bf16[896,512]{1,0:T(8,128)(2,1)S(1)}, bf16[896,512]{1,0:T(8,128)(2,1)}, u32[]{:S(2)}, u32[]{:S(2)}) collective-permute-start(bf16[896,512]{1,0:T(8,128)(2,1)S(1)} %collective-permute-done.1.refs_2_), channel_id=1, source_target_pairs={{8,0},{12,4},{16,8},{20,12},{24,16},{28,20},{9,1},{13,5},{17,9},{2... | collective-permute-start | bytes 2752520 | tf_op jit(solution)/shard_map/ppermute | solution.py:369
  60.1 9.8 %collective-permute-start.13 = (bf16[896,512]{1,0:T(8,128)(2,1)}, bf16[896,512]{1,0:T(8,128)(2,1)}, u32[]{:S(2)}, u32[]{:S(2)}) collective-permute-start(bf16[896,512]{1,0:T(8,128)(2,1)} %get-tuple-element.76.refs_0_), channel_id=1, source_target_pairs={{0,4},{4,0},{8,12},{12,8},{16,20},{20,16},{24,28},{28,24},{1,5},{5... | collective-permute-start | bytes 2752520 | tf_op jit(solution)/shard_map/ppermute | solution.py:376
  61.4 9.9 %collective-permute-start.11 = (bf16[896,512]{1,0:T(8,128)(2,1)}, bf16[896,512]{1,0:T(8,128)(2,1)S(1)}, u32[]{:S(2)}, u32[]{:S(2)}) collective-permute-start(bf16[896,512]{1,0:T(8,128)(2,1)} %collective-permute-done.3.refs_4_), channel_id=1, source_target_pairs={{0,4},{4,0},{8,12},{12,8},{16,20},{20,16},{24,28},{28,24},{1,5},{5... | collective-permute-start | bytes 2752520 | tf_op jit(solution)/shard_map/ppermute | solution.py:376
  61.4 32.0 %collective-permute-start.12 = (bf16[896,512]{1,0:T(8,128)(2,1)}, bf16[896,512]{1,0:T(8,128)(2,1)}, u32[]{:S(2)}, u32[]{:S(2)}) collective-permute-start(bf16[896,512]{1,0:T(8,128)(2,1)} %collective-permute-done.4.refs_6_), channel_id=1, source_target_pairs={{0,4},{4,0},{8,12},{12,8},{16,20},{20,16},{24,28},{28,24},{1,5},{5... | collective-permute-start | bytes 2752520 | tf_op jit(solution)/shard_map/ppermute | solution.py:376
  64.5 28.9 %copy-start.17 = (bf16[896,512]{1,0:T(8,128)(2,1)S(1)}, bf16[896,512]{1,0:T(8,128)(2,1)}, u32[]{:S(2)}) copy-start(bf16[896,512]{1,0:T(8,128)(2,1)} %copy-done.16) | copy-start | bytes 2752516
  64.5 28.9 %copy-start.19 = (bf16[896,512]{1,0:T(8,128)(2,1)S(1)}, bf16[896,512]{1,0:T(8,128)(2,1)}, u32[]{:S(2)}) copy-start(bf16[896,512]{1,0:T(8,128)(2,1)} %copy-done.18) | copy-start | bytes 2752516
  64.5 42.1 %collective-permute-start.10 = (bf16[896,512]{1,0:T(8,128)(2,1)}, bf16[896,512]{1,0:T(8,128)(2,1)S(1)}, u32[]{:S(2)}, u32[]{:S(2)}) collective-permute-start(bf16[896,512]{1,0:T(8,128)(2,1)} %get-tuple-element.76.refs_0_), channel_id=1, source_target_pairs={{8,0},{12,4},{16,8},{20,12},{24,16},{28,20},{9,1},{13,5},{17,9},{2... | collective-permute-start | bytes 2752520 | tf_op jit(solution)/shard_map/ppermute | solution.py:369
  65.9 40.7 %collective-permute-start.7 = (bf16[896,512]{1,0:T(8,128)(2,1)}, bf16[896,512]{1,0:T(8,128)(2,1)S(1)}, u32[]{:S(2)}, u32[]{:S(2)}) collective-permute-start(bf16[896,512]{1,0:T(8,128)(2,1)} %collective-permute-done.3.refs_4_), channel_id=1, source_target_pairs={{0,8},{4,12},{8,16},{12,20},{16,24},{20,28},{1,9},{5,13},{9,17},{1... | collective-permute-start | bytes 2752520 | tf_op jit(solution)/shard_map/ppermute | solution.py:369
  70.0 38.4 %collective-permute-start.8 = (bf16[896,512]{1,0:T(8,128)(2,1)}, bf16[896,512]{1,0:T(8,128)(2,1)S(1)}, u32[]{:S(2)}, u32[]{:S(2)}) collective-permute-start(bf16[896,512]{1,0:T(8,128)(2,1)} %collective-permute-done.4.refs_6_), channel_id=1, source_target_pairs={{8,0},{12,4},{16,8},{20,12},{24,16},{28,20},{9,1},{13,5},{17,9},{2... | collective-permute-start | bytes 2752520 | tf_op jit(solution)/shard_map/ppermute | solution.py:369
  72.2 37.1 %collective-permute-start.9 = (bf16[896,512]{1,0:T(8,128)(2,1)}, bf16[896,512]{1,0:T(8,128)(2,1)S(1)}, u32[]{:S(2)}, u32[]{:S(2)}) collective-permute-start(bf16[896,512]{1,0:T(8,128)(2,1)} %get-tuple-element.76.refs_0_), channel_id=1, source_target_pairs={{0,8},{4,12},{8,16},{12,20},{16,24},{20,28},{1,9},{5,13},{9,17},{1... | collective-permute-start | bytes 2752520 | tf_op jit(solution)/shard_map/ppermute | solution.py:369
  109.3 56.9 %copy-start.10 = (bf16[896,512]{1,0:T(8,128)(2,1)}, bf16[896,512]{1,0:T(8,128)(2,1)S(1)}, u32[]{:S(2)}) copy-start(bf16[896,512]{1,0:T(8,128)(2,1)S(1)} %collective-permute-done.9.refs_0_) | copy-start | bytes 2752516
  109.3 8.1 %collective-permute-start.14 = (bf16[896,512]{1,0:T(8,128)(2,1)S(1)}, bf16[896,512]{1,0:T(8,128)(2,1)S(1)}, u32[]{:S(2)}, u32[]{:S(2)}) collective-permute-start(bf16[896,512]{1,0:T(8,128)(2,1)S(1)} %collective-permute-done.7.refs_8_), channel_id=1, source_target_pairs={{0,4},{4,0},{8,12},{12,8},{16,20},{20,16},{24,28},{28,24},{1,5},{5... | collective-permute-start | bytes 2752520 | tf_op jit(solution)/shard_map/ppermute | solution.py:376
  110.4 7.1 %collective-permute-start.15 = (bf16[896,512]{1,0:T(8,128)(2,1)S(1)}, bf16[896,512]{1,0:T(8,128)(2,1)S(1)}, u32[]{:S(2)}, u32[]{:S(2)}) collective-permute-start(bf16[896,512]{1,0:T(8,128)(2,1)S(1)} %collective-permute-done.8.refs_10_), channel_id=1, source_target_pairs={{0,4},{4,0},{8,12},{12,8},{16,20},{20,16},{24,28},{28,24},{1,5},{5... | collective-permute-start | bytes 2752520 | tf_op jit(solution)/shard_map/ppermute | solution.py:376
  110.4 26.9 %collective-permute-start.19 = (bf16[896,512]{1,0:T(8,128)(2,1)S(1)}, bf16[896,512]{1,0:T(8,128)(2,1)}, u32[]{:S(2)}, u32[]{:S(2)}) collective-permute-start(bf16[896,512]{1,0:T(8,128)(2,1)S(1)} %collective-permute-done.9.refs_0_), channel_id=1, source_target_pairs={{0,8},{4,12},{8,16},{12,20},{16,24},{20,28},{1,9},{5,13},{9,17},{1... | collective-permute-start | bytes 2752520 | tf_op jit(solution)/shard_map/ppermute | solution.py:369
  115.4 30.4 %collective-permute-start.23 = (bf16[896,512]{1,0:T(8,128)(2,1)S(1)}, bf16[896,512]{1,0:T(8,128)(2,1)S(1)}, u32[]{:S(2)}, u32[]{:S(2)}) collective-permute-start(bf16[896,512]{1,0:T(8,128)(2,1)S(1)} %collective-permute-done.9.refs_0_), channel_id=1, source_target_pairs={{0,4},{4,0},{8,12},{12,8},{16,20},{20,16},{24,28},{28,24},{1,5},{5... | collective-permute-start | bytes 2752520 | tf_op jit(solution)/shard_map/ppermute | solution.py:376
  116.2 24.0 %collective-permute-start.20 = (bf16[896,512]{1,0:T(8,128)(2,1)S(1)}, bf16[896,512]{1,0:T(8,128)(2,1)}, u32[]{:S(2)}, u32[]{:S(2)}) collective-permute-start(bf16[896,512]{1,0:T(8,128)(2,1)S(1)} %collective-permute-done.10.refs_2_), channel_id=1, source_target_pairs={{8,0},{12,4},{16,8},{20,12},{24,16},{28,20},{9,1},{13,5},{17,9},{2... | collective-permute-start | bytes 2752520 | tf_op jit(solution)/shard_map/ppermute | solution.py:369
  117.4 29.7 %collective-permute-start.24 = (bf16[896,512]{1,0:T(8,128)(2,1)S(1)}, bf16[896,512]{1,0:T(8,128)(2,1)}, u32[]{:S(2)}, u32[]{:S(2)}) collective-permute-start(bf16[896,512]{1,0:T(8,128)(2,1)S(1)} %collective-permute-done.10.refs_2_), channel_id=1, source_target_pairs={{0,4},{4,0},{8,12},{12,8},{16,20},{20,16},{24,28},{28,24},{1,5},{5... | collective-permute-start | bytes 2752520 | tf_op jit(solution)/shard_map/ppermute | solution.py:376
  140.1 9.2 %collective-permute-start.25 = (bf16[896,512]{1,0:T(8,128)(2,1)}, bf16[896,512]{1,0:T(8,128)(2,1)}, u32[]{:S(2)}, u32[]{:S(2)}) collective-permute-start(bf16[896,512]{1,0:T(8,128)(2,1)} %collective-permute-done.19.refs_4_), channel_id=1, source_target_pairs={{0,4},{4,0},{8,12},{12,8},{16,20},{20,16},{24,28},{28,24},{1,5},{5... | collective-permute-start | bytes 2752520 | tf_op jit(solution)/shard_map/ppermute | solution.py:376
  140.9 8.7 %collective-permute-start.26 = (bf16[896,512]{1,0:T(8,128)(2,1)}, bf16[896,512]{1,0:T(8,128)(2,1)}, u32[]{:S(2)}, u32[]{:S(2)}) collective-permute-start(bf16[896,512]{1,0:T(8,128)(2,1)} %collective-permute-done.20.refs_6_), channel_id=1, source_target_pairs={{0,4},{4,0},{8,12},{12,8},{16,20},{20,16},{24,28},{28,24},{1,5},{5... | collective-permute-start | bytes 2752520 | tf_op jit(solution)/shard_map/ppermute | solution.py:376
  143.5 38.9 %collective-permute-start.21 = (bf16[896,512]{1,0:T(8,128)(2,1)}, bf16[896,512]{1,0:T(8,128)(2,1)S(1)}, u32[]{:S(2)}, u32[]{:S(2)}) collective-permute-start(bf16[896,512]{1,0:T(8,128)(2,1)} %collective-permute-done.19.refs_4_), channel_id=1, source_target_pairs={{0,8},{4,12},{8,16},{12,20},{16,24},{20,28},{1,9},{5,13},{9,17},{1... | collective-permute-start | bytes 2752520 | tf_op jit(solution)/shard_map/ppermute | solution.py:369
  145.8 36.6 %collective-permute-start.22 = (bf16[896,512]{1,0:T(8,128)(2,1)}, bf16[896,512]{1,0:T(8,128)(2,1)S(1)}, u32[]{:S(2)}, u32[]{:S(2)}) collective-permute-start(bf16[896,512]{1,0:T(8,128)(2,1)} %collective-permute-done.20.refs_6_), channel_id=1, source_target_pairs={{8,0},{12,4},{16,8},{20,12},{24,16},{28,20},{9,1},{13,5},{17,9},{2... | collective-permute-start | bytes 2752520 | tf_op jit(solution)/shard_map/ppermute | solution.py:369
  147.1 35.3 %collective-permute-start.18 = (f16[912,512]{1,0:T(8,128)(2,1)}, f16[912,512]{1,0:T(8,128)(2,1)S(1)}, u32[]{:S(2)}, u32[]{:S(2)}) collective-permute-start(f16[912,512]{1,0:T(8,128)(2,1)} %pad_maximum_fusion.4), channel_id=1, source_target_pairs={{0,3},{1,0},{2,1},{3,2},{4,7},{5,4},{6,5},{7,6},{8,11},{9,8},{10,9... | collective-permute-start | bytes 2801672 | tf_op jit(solution)/shard_map/ppermute | solution.py:452
  149.4 33.1 %collective-permute-start.17 = (f16[912,512]{1,0:T(8,128)(2,1)}, f16[912,512]{1,0:T(8,128)(2,1)S(1)}, u32[]{:S(2)}, u32[]{:S(2)}) collective-permute-start(f16[912,512]{1,0:T(8,128)(2,1)} %pad_maximum_fusion.3), channel_id=1, source_target_pairs={{0,2},{1,3},{2,0},{3,1},{4,6},{5,7},{6,4},{7,5},{8,10},{9,11},{10,... | collective-permute-start | bytes 2801672 | tf_op jit(solution)/shard_map/ppermute | solution.py:452
  149.6 40.6 %collective-permute-start.16 = (f16[912,512]{1,0:T(8,128)(2,1)}, f16[912,512]{1,0:T(8,128)(2,1)S(1)}, u32[]{:S(2)}, u32[]{:S(2)}) collective-permute-start(f16[912,512]{1,0:T(8,128)(2,1)} %pad_maximum_fusion.2), channel_id=1, source_target_pairs={{0,1},{1,2},{2,3},{3,0},{4,5},{5,6},{6,7},{7,4},{8,9},{9,10},{10,1... | collective-permute-start | bytes 2801672 | tf_op jit(solution)/shard_map/ppermute | solution.py:452
  191.0 7.7 %collective-permute-start.28 = (bf16[896,512]{1,0:T(8,128)(2,1)S(1)}, bf16[896,512]{1,0:T(8,128)(2,1)S(1)}, u32[]{:S(2)}, u32[]{:S(2)}) collective-permute-start(bf16[896,512]{1,0:T(8,128)(2,1)S(1)} %collective-permute-done.21.refs_8_), channel_id=1, source_target_pairs={{0,4},{4,0},{8,12},{12,8},{16,20},{20,16},{24,28},{28,24},{1,5},{5... | collective-permute-start | bytes 2752520 | tf_op jit(solution)/shard_map/ppermute | solution.py:376
  193.6 5.1 %collective-permute-start.29 = (bf16[896,512]{1,0:T(8,128)(2,1)S(1)}, bf16[896,512]{1,0:T(8,128)(2,1)S(1)}, u32[]{:S(2)}, u32[]{:S(2)}) collective-permute-start(bf16[896,512]{1,0:T(8,128)(2,1)S(1)} %collective-permute-done.22.refs_10_), channel_id=1, source_target_pairs={{0,4},{4,0},{8,12},{12,8},{16,20},{20,16},{24,28},{28,24},{1,5},{5... | collective-permute-start | bytes 2752520 | tf_op jit(solution)/shard_map/ppermute | solution.py:376
  198.2 11.4 %collective-permute-start.27 = (f32[256,512]{1,0:T(8,128)S(1)}, f32[256,512]{1,0:T(8,128)S(1)}, u32[]{:S(2)}, u32[]{:S(2)}) collective-permute-start(f32[256,512]{1,0:T(8,128)S(1)} %constant_dynamic-slice_fusion.13), channel_id=1, source_target_pairs={{0,4},{4,0},{8,12},{12,8},{16,20},{20,16},{24,28},{28,24},{1,5},{5... | collective-permute-start | bytes 1572872 | tf_op jit(solution)/shard_map/ppermute | solution.py:492
  207.8 60.8 %collective-permute-start.31 = (f16[912,512]{1,0:T(8,128)(2,1)}, f16[912,512]{1,0:T(8,128)(2,1)}, u32[]{:S(2)}, u32[]{:S(2)}) collective-permute-start(f16[912,512]{1,0:T(8,128)(2,1)} %pad_maximum_fusion.6), channel_id=1, source_target_pairs={{0,2},{1,3},{2,0},{3,1},{4,6},{5,7},{6,4},{7,5},{8,10},{9,11},{10,... | collective-permute-start | bytes 2801672 | tf_op jit(solution)/shard_map/ppermute | solution.py:452
  209.3 59.4 %collective-permute-start.30 = (f16[912,512]{1,0:T(8,128)(2,1)}, f16[912,512]{1,0:T(8,128)(2,1)}, u32[]{:S(2)}, u32[]{:S(2)}) collective-permute-start(f16[912,512]{1,0:T(8,128)(2,1)} %pad_maximum_fusion.5), channel_id=1, source_target_pairs={{0,1},{1,2},{2,3},{3,0},{4,5},{5,6},{6,7},{7,4},{8,9},{9,10},{10,1... | collective-permute-start | bytes 2801672 | tf_op jit(solution)/shard_map/ppermute | solution.py:452
  218.7 49.9 %collective-permute-start.32 = (f16[912,512]{1,0:T(8,128)(2,1)S(1)}, f16[912,512]{1,0:T(8,128)(2,1)}, u32[]{:S(2)}, u32[]{:S(2)}) collective-permute-start(f16[912,512]{1,0:T(8,128)(2,1)S(1)} %pad_maximum_fusion.7), channel_id=1, source_target_pairs={{0,3},{1,0},{2,1},{3,2},{4,7},{5,4},{6,5},{7,6},{8,11},{9,8},{10,9... | collective-permute-start | bytes 2801672 | tf_op jit(solution)/shard_map/ppermute | solution.py:452
  221.6 33.6 %collective-permute-start.33 = (f32[64,512]{1,0:T(8,128)S(1)}, f32[64,512]{1,0:T(8,128)S(1)}, u32[]{:S(2)}, u32[]{:S(2)}) collective-permute-start(f32[64,512]{1,0:T(8,128)S(1)} %get-tuple-element.159), channel_id=1, source_target_pairs={{0,1},{1,2},{2,3},{3,0},{4,5},{5,6},{6,7},{7,4},{8,9},{9,10},{10,1... | collective-permute-start | bytes 393224 | tf_op jit(solution)/shard_map/ppermute | solution.py:492
  221.7 33.6 %collective-permute-start.34 = (f32[64,512]{1,0:T(8,128)}, f32[64,512]{1,0:T(8,128)}, u32[]{:S(2)}, u32[]{:S(2)}) collective-permute-start(f32[64,512]{1,0:T(8,128)} %get-tuple-element.158), channel_id=1, source_target_pairs={{0,2},{1,3},{2,0},{3,1},{4,6},{5,7},{6,4},{7,5},{8,10},{9,11},{10,... | collective-permute-start | bytes 393224 | tf_op jit(solution)/shard_map/ppermute | solution.py:492
  255.2 3.9 collective-permute-start.35
  260.8 4.6 %collective-permute-start.36 = (f32[16,512]{1,0:T(8,128)S(1)}, f32[16,512]{1,0:T(8,128)S(1)}, u32[]{:S(2)}, u32[]{:S(2)}) collective-permute-start(f32[16,512]{1,0:T(8,128)S(1)} %get-tuple-element.165), channel_id=1, source_target_pairs={{0,8},{4,12},{8,16},{12,20},{16,24},{20,28},{24,0},{28,4},{1,9},{5... | collective-permute-start | bytes 98312 | tf_op jit(solution)/shard_map/ppermute | solution.py:492
  264.0 3.8 collective-permute-start.37
  265.4 3.2 collective-permute-start.38
  278.9 12.1 %collective-permute-start.42 = (f32[512,512]{1,0:T(8,128)S(1)}, f32[512,512]{1,0:T(8,128)}, u32[]{:S(2)}, u32[]{:S(2)}) collective-permute-start(f32[512,512]{1,0:T(8,128)S(1)} %constant_dynamic-slice_fusion.6), channel_id=1, source_target_pairs={{0,4},{4,0},{8,12},{12,8},{16,20},{20,16},{24,28},{28,24},{1,5},{5... | collective-permute-start | bytes 3145736 | tf_op jit(solution)/shard_map/ppermute | solution.py:492
  284.3 4.6 %collective-permute-start.39 = (f32[16,512]{1,0:T(8,128)S(1)}, f32[16,512]{1,0:T(8,128)S(1)}, u32[]{:S(2)}, u32[]{:S(2)}) collective-permute-start(f32[16,512]{1,0:T(8,128)S(1)} %get-tuple-element.146), channel_id=1, source_target_pairs={{0,8},{4,12},{8,16},{12,20},{16,24},{20,28},{24,0},{28,4},{1,9},{5... | collective-permute-start | bytes 98312 | tf_op jit(solution)/shard_map/ppermute | solution.py:512
  285.9 5.1 %collective-permute-start.40 = (f32[16,512]{1,0:T(8,128)S(1)}, f32[16,512]{1,0:T(8,128)S(1)}, u32[]{:S(2)}, u32[]{:S(2)}) collective-permute-start(f32[16,512]{1,0:T(8,128)S(1)} %get-tuple-element.146), channel_id=1, source_target_pairs={{0,16},{4,20},{8,24},{12,28},{16,0},{20,4},{24,8},{28,12},{1,17},{... | collective-permute-start | bytes 98312 | tf_op jit(solution)/shard_map/ppermute | solution.py:512
  287.1 3.9 collective-permute-start.41
  292.8 20.4 %collective-permute-start.46 = (f32[128,512]{1,0:T(8,128)S(1)}, f32[128,512]{1,0:T(8,128)S(1)}, u32[]{:S(2)}, u32[]{:S(2)}) collective-permute-start(f32[128,512]{1,0:T(8,128)S(1)} %get-tuple-element.156), channel_id=1, source_target_pairs={{0,1},{1,2},{2,3},{3,0},{4,5},{5,6},{6,7},{7,4},{8,9},{9,10},{10,1... | collective-permute-start | bytes 786440 | tf_op jit(solution)/shard_map/ppermute | solution.py:492
  293.6 10.1 %collective-permute-start.43 = (f32[64,512]{1,0:T(8,128)S(1)}, f32[64,512]{1,0:T(8,128)S(1)}, u32[]{:S(2)}, u32[]{:S(2)}) collective-permute-start(f32[64,512]{1,0:T(8,128)S(1)} %constant_dynamic-update-slice_fusion.16), channel_id=1, source_target_pairs={{0,1},{1,2},{2,3},{3,0},{4,5},{5,6},{6,7},{7,4},{8,9},{9,10},{10,1... | collective-permute-start | bytes 393224 | tf_op jit(solution)/shard_map/ppermute | solution.py:512
  295.3 17.9 %collective-permute-start.47 = (f32[128,512]{1,0:T(8,128)S(1)}, f32[128,512]{1,0:T(8,128)S(1)}, u32[]{:S(2)}, u32[]{:S(2)}) collective-permute-start(f32[128,512]{1,0:T(8,128)S(1)} %get-tuple-element.155), channel_id=1, source_target_pairs={{0,2},{1,3},{2,0},{3,1},{4,6},{5,7},{6,4},{7,5},{8,10},{9,11},{10,... | collective-permute-start | bytes 786440 | tf_op jit(solution)/shard_map/ppermute | solution.py:492
  295.6 17.7 %collective-permute-start.48 = (f32[128,512]{1,0:T(8,128)S(1)}, f32[128,512]{1,0:T(8,128)S(1)}, u32[]{:S(2)}, u32[]{:S(2)}) collective-permute-start(f32[128,512]{1,0:T(8,128)S(1)} %get-tuple-element.154), channel_id=1, source_target_pairs={{0,3},{1,0},{2,1},{3,2},{4,7},{5,4},{6,5},{7,6},{8,11},{9,8},{10,9... | collective-permute-start | bytes 786440 | tf_op jit(solution)/shard_map/ppermute | solution.py:492
  296.6 16.6 %collective-permute-start.44 = (f32[64,512]{1,0:T(8,128)S(1)}, f32[64,512]{1,0:T(8,128)S(1)}, u32[]{:S(2)}, u32[]{:S(2)}) collective-permute-start(f32[64,512]{1,0:T(8,128)S(1)} %constant_dynamic-update-slice_fusion.16), channel_id=1, source_target_pairs={{0,2},{1,3},{2,0},{3,1},{4,6},{5,7},{6,4},{7,5},{8,10},{9,11},{10,... | collective-permute-start | bytes 393224 | tf_op jit(solution)/shard_map/ppermute | solution.py:512
  303.6 9.6 %collective-permute-start.45 = (f32[64,512]{1,0:T(8,128)S(1)}, f32[64,512]{1,0:T(8,128)S(1)}, u32[]{:S(2)}, u32[]{:S(2)}) collective-permute-start(f32[64,512]{1,0:T(8,128)S(1)} %constant_dynamic-update-slice_fusion.16), channel_id=1, source_target_pairs={{0,3},{1,0},{2,1},{3,2},{4,7},{5,4},{6,5},{7,6},{8,11},{9,8},{10,9... | collective-permute-start | bytes 393224 | tf_op jit(solution)/shard_map/ppermute | solution.py:512
  314.1 10.1 %collective-permute-start.49 = (f32[256,512]{1,0:T(8,128)S(1)}, f32[256,512]{1,0:T(8,128)}, u32[]{:S(2)}, u32[]{:S(2)}) collective-permute-start(f32[256,512]{1,0:T(8,128)S(1)} %constant_dynamic-update-slice_fusion.12), channel_id=1, source_target_pairs={{0,4},{4,0},{8,12},{12,8},{16,20},{20,16},{24,28},{28,24},{1,5},{5... | collective-permute-start | bytes 1572872 | tf_op jit(solution)/shard_map/ppermute | solution.py:512
  315.9 5.6 %collective-permute-start.50 = (f32[32,512]{1,0:T(8,128)S(1)}, f32[32,512]{1,0:T(8,128)S(1)}, u32[]{:S(2)}, u32[]{:S(2)}) collective-permute-start(f32[32,512]{1,0:T(8,128)S(1)} %get-tuple-element.162), channel_id=1, source_target_pairs={{0,8},{4,12},{8,16},{12,20},{16,24},{20,28},{24,0},{28,4},{1,9},{5... | collective-permute-start | bytes 196616 | tf_op jit(solution)/shard_map/ppermute | solution.py:492
  316.7 7.5 %collective-permute-start.51 = (f32[32,512]{1,0:T(8,128)S(1)}, f32[32,512]{1,0:T(8,128)S(1)}, u32[]{:S(2)}, u32[]{:S(2)}) collective-permute-start(f32[32,512]{1,0:T(8,128)S(1)} %get-tuple-element.161), channel_id=1, source_target_pairs={{0,16},{4,20},{8,24},{12,28},{16,0},{20,4},{24,8},{28,12},{1,17},{... | collective-permute-start | bytes 196616 | tf_op jit(solution)/shard_map/ppermute | solution.py:492
  317.9 6.3 %collective-permute-start.52 = (f32[32,512]{1,0:T(8,128)S(1)}, f32[32,512]{1,0:T(8,128)S(1)}, u32[]{:S(2)}, u32[]{:S(2)}) collective-permute-start(f32[32,512]{1,0:T(8,128)S(1)} %get-tuple-element.160), channel_id=1, source_target_pairs={{0,24},{4,28},{8,0},{12,4},{16,8},{20,12},{24,16},{28,20},{1,25},{... | collective-permute-start | bytes 196616 | tf_op jit(solution)/shard_map/ppermute | solution.py:492
  325.4 31.5 %collective-permute-start.53 = (f32[32,512]{1,0:T(8,128)S(1)}, f32[32,512]{1,0:T(8,128)S(1)}, u32[]{:S(2)}, u32[]{:S(2)}) collective-permute-start(f32[32,512]{1,0:T(8,128)S(1)} %get-tuple-element.144), channel_id=1, source_target_pairs={{0,8},{4,12},{8,16},{12,20},{16,24},{20,28},{24,0},{28,4},{1,9},{5... | collective-permute-start | bytes 196616 | tf_op jit(solution)/shard_map/ppermute | solution.py:512
  327.1 29.8 %collective-permute-start.54 = (f32[32,512]{1,0:T(8,128)S(1)}, f32[32,512]{1,0:T(8,128)S(1)}, u32[]{:S(2)}, u32[]{:S(2)}) collective-permute-start(f32[32,512]{1,0:T(8,128)S(1)} %get-tuple-element.144), channel_id=1, source_target_pairs={{0,16},{4,20},{8,24},{12,28},{16,0},{20,4},{24,8},{28,12},{1,17},{... | collective-permute-start | bytes 196616 | tf_op jit(solution)/shard_map/ppermute | solution.py:512
  328.3 28.7 %collective-permute-start.55 = (f32[32,512]{1,0:T(8,128)S(1)}, f32[32,512]{1,0:T(8,128)S(1)}, u32[]{:S(2)}, u32[]{:S(2)}) collective-permute-start(f32[32,512]{1,0:T(8,128)S(1)} %get-tuple-element.144), channel_id=1, source_target_pairs={{0,24},{4,28},{8,0},{12,4},{16,8},{20,12},{24,16},{28,20},{1,25},{... | collective-permute-start | bytes 196616 | tf_op jit(solution)/shard_map/ppermute | solution.py:512
  357.0 7.6 %collective-permute-start.56 = (f32[128,512]{1,0:T(8,128)S(1)}, f32[128,512]{1,0:T(8,128)S(1)}, u32[]{:S(2)}, u32[]{:S(2)}) collective-permute-start(f32[128,512]{1,0:T(8,128)S(1)} %constant_dynamic-update-slice_fusion.6), channel_id=1, source_target_pairs={{0,1},{1,2},{2,3},{3,0},{4,5},{5,6},{6,7},{7,4},{8,9},{9,10},{10,1... | collective-permute-start | bytes 786440 | tf_op jit(solution)/shard_map/ppermute | solution.py:512
  358.6 13.2 %collective-permute-start.57 = (f32[128,512]{1,0:T(8,128)S(1)}, f32[128,512]{1,0:T(8,128)S(1)}, u32[]{:S(2)}, u32[]{:S(2)}) collective-permute-start(f32[128,512]{1,0:T(8,128)S(1)} %constant_dynamic-update-slice_fusion.6), channel_id=1, source_target_pairs={{0,2},{1,3},{2,0},{3,1},{4,6},{5,7},{6,4},{7,5},{8,10},{9,11},{10,... | collective-permute-start | bytes 786440 | tf_op jit(solution)/shard_map/ppermute | solution.py:512
  359.5 12.3 %collective-permute-start.58 = (f32[128,512]{1,0:T(8,128)S(1)}, f32[128,512]{1,0:T(8,128)S(1)}, u32[]{:S(2)}, u32[]{:S(2)}) collective-permute-start(f32[128,512]{1,0:T(8,128)S(1)} %constant_dynamic-update-slice_fusion.6), channel_id=1, source_target_pairs={{0,3},{1,0},{2,1},{3,2},{4,7},{5,4},{6,5},{7,6},{8,11},{9,8},{10,9... | collective-permute-start | bytes 786440 | tf_op jit(solution)/shard_map/ppermute | solution.py:512
  371.9 3.2 collective-permute-start.59
  (33 other events, 280.2 us)

commit v2 on v1

--- a/solution.py
+++ b/solution.py
@@ -253,6 +253,21 @@
     return jnp.dot(a, b, precision=HIGHEST, preferred_element_type=jnp.float32)
 
 
+def halves(x):
+    high = x.astype(jnp.bfloat16)
+    return high, (x - high.astype(jnp.float32)).astype(jnp.bfloat16)
+
+
+def mul_halves(a, b):
+    a_high, a_low = halves(a)
+    b_high, b_low = halves(b)
+
+    def nn(x, y):
+        return jnp.dot(x, y, preferred_element_type=jnp.float32)
+
+    return nn(a_high, b_high) + (nn(a_high, b_low) + nn(a_low, b_high))
+
+
 def column_kernel(scale, before, width, gram_ref, *refs):
     factor_ref, inverse_ref = refs[-2:]
     block = gram_ref[before:, :] * scale
@@ -280,7 +295,7 @@
     factor_ref[before:, :] = factor
     inverse_ref[:, before:] = inverse
     if before:
-        inverse_ref[:, :before] = -mul(mul(inverse, above_t), refs[0][...])
+        inverse_ref[:, :before] = -mul_halves(mul(inverse, above_t), refs[0][...])
 
 
 def factor_column(gram, inverse_before, scale):
@@ -298,11 +313,6 @@
         compiler_params=pltpu.CompilerParams(vmem_limit_bytes=32 * 1024 * 1024),
         cost_estimate=pl.CostEstimate(flops=16_000_000_000, bytes_accessed=4_000_000, transcendentals=0),
     )(*operands)
-
-
-def halves(x):
-    high = x.astype(jnp.bfloat16)
-    return high, (x - high.astype(jnp.float32)).astype(jnp.bfloat16)
 
 
 def basis_kernel(x_ref, rows_ref, *refs):

time: 429 us -> 428 us (level)
  no operation moved by 1% of the time
where the time goes in v2:
time: 428 us; the launch traced here: 420 us
  Pallas kernels  176 us (41%)
  waiting for transfers between devices  91.1 us (21%)
  starting transfers between devices  77.1 us (18%)
  local copies, waits for them, and re-layouts  42.2 us (10%)
  other arithmetic  25.7 us (6%)
  matrix products  5.31 us (1%)
    pallas_call x9, Pallas kernels, level_product(): pl.pallas_call(functools.partial(level_kernel, pieces, len(blocks) // 2,...  106 us
    pallas_call x4, Pallas kernels, factor_column(): pl.pallas_call(functools.partial(column_kernel, scale, before, width), ou...  63.6 us
    ppermute x14, waiting for transfers between devices, task(): put(('add', c, step), lax.ppermute(piece, axis, perm(step)), line.now + 1)  44.4 us
    ppermute x12, starting transfers between devices, task(): put((way, c, step), lax.ppermute(source, 'row', perm), arrival[c, step])  31.9 us
    ppermute x14, waiting for transfers between devices, task(): lax.ppermute(get(('sum', c)), axis, perm(step))  29.7 us
    unnamed x74, local copies, waits for them, and re-layouts  26.1 us
    ppermute x14, starting transfers between devices, task(): put(('add', c, step), lax.ppermute(piece, axis, perm(step)), line.now + 1)  16.2 us
    ppermute x14, starting transfers between devices, task(): lax.ppermute(get(('sum', c)), axis, perm(step))  15.1 us
  transfers between devices with their start and end apart: 60, of which 18 were waited for; matrix products, arithmetic and copies ran while one was open for 7% of the time, Pallas kernels for 32%

profile of v2, /device:TPU:1, one launch (start us, length us, event | category | flops | bytes accessed | tf_op | source)
XLA Modules:
  0.0 419.5 jit_solution(4176765289458678444)
XLA Ops:
  0.7 2.5 fusion.29
  3.2 4.7 %collective-permute-start = (bf16[896,512]{1,0:T(8,128)(2,1)S(1)}, bf16[896,512]{1,0:T(8,128)(2,1)S(1)}, u32[]{:S(2)}, u32[]{:S(2)}) collective-permute-start(bf16[896,512]{1,0:T(8,128)(2,1)S(1)} %get-tuple-element.152.refs_0_), channel_id=1, source_target_pairs={{0,8},{4,12},{8,16},{12,20},{16,24},{20,28},{1,9},{5,13},{9,17},{1... | collective-permute-start | bytes 2752520 | tf_op jit(solution)/shard_map/ppermute | solution.py:379
  11.8 13.0 %shard_map.167.refs_4_ = f32[4,896,512]{2,1,0:T(8,128)S(1)} custom-call(s32[7]{0:T(128)S(1)} %stack.36.place_ref, bf16[3584,7168]{1,0:T(8,128)(2,1)} %factor_ref.17, bf16[896,512]{1,0:T(8,128)(2,1)S(1)} %get-tuple-element.152.refs_0_, bf16[896,512]{1,0:T(8,128)(2,1)} %collective-permute-done.2.refs_1_), custom_call_target="tpu_custom_call" | custom-call | flops 6576668672 | bytes 12845056 | tf_op jit(solution)/shard_map/pallas_call | solution.py:90
  24.9 3.0 copy-done
  27.8 3.6 collective-permute-done.1.refs_2_
  32.6 4.1 collective-permute-start.3
  39.3 1.4 stack.34.place_ref
  40.7 3.4 copy-done.1
  44.1 13.1 %shard_map.168.refs_8_ = f32[4,896,512]{2,1,0:T(8,128)S(1)} custom-call(s32[7]{0:T(128)S(1)} %stack.37.place_ref, bf16[3584,7168]{1,0:T(8,128)(2,1)} %factor_ref.17, bf16[896,512]{1,0:T(8,128)(2,1)S(1)} %collective-permute-done.refs_0_, bf16[896,512]{1,0:T(8,128)(2,1)S(1)} %collective-permute-done.5.refs_1_, ...), custom_call_target="tpu_custom_call", output_to_operand_aliasing={{}: (6, {})} | custom-call | flops 6576668672 | bytes 12845056 | tf_op jit(solution)/shard_map/pallas_call | solution.py:90
  57.2 2.9 copy-done.2
  64.5 1.4 collective-permute-start.10
  65.9 4.0 collective-permute-start.7
  72.2 4.0 collective-permute-start.9
  76.3 14.1 %shard_map.170.refs_4_ = f32[4,896,512]{2,1,0:T(8,128)S(1)} custom-call(s32[7]{0:T(128)S(1)} %stack.36.place_ref, bf16[3584,7168]{1,0:T(8,128)(2,1)} %factor_ref.17, bf16[896,512]{1,0:T(8,128)(2,1)} %get-tuple-element.76.refs_0_, bf16[896,512]{1,0:T(8,128)(2,1)} %collective-permute-done.13.refs_1_), custom_call_target="tpu_custom_call" | custom-call | flops 6576668672 | bytes 12845056 | tf_op jit(solution)/shard_map/pallas_call | solution.py:90
  90.4 3.0 copy-done.5
  93.4 13.2 %shard_map.169.refs_12_ = f32[4,896,512]{2,1,0:T(8,128)S(1)} custom-call(s32[7]{0:T(128)S(1)} %stack.34.place_ref, bf16[3584,7168]{1,0:T(8,128)(2,1)} %factor_ref.17, bf16[896,512]{1,0:T(8,128)(2,1)S(1)} %collective-permute-done.refs_0_, bf16[896,512]{1,0:T(8,128)(2,1)S(1)} %copy-done.19, ...), custom_call_target="tpu_custom_call", output_to_operand_aliasing={{}: (10, {})} | custom-call | flops 6576668672 | bytes 12845056 | tf_op jit(solution)/shard_map/pallas_call | solution.py:90
  106.6 1.7 collective-permute-done.8.refs_10_
  110.4 4.9 %collective-permute-start.19 = (bf16[896,512]{1,0:T(8,128)(2,1)S(1)}, bf16[896,512]{1,0:T(8,128)(2,1)}, u32[]{:S(2)}, u32[]{:S(2)}) collective-permute-start(bf16[896,512]{1,0:T(8,128)(2,1)S(1)} %collective-permute-done.9.refs_0_), channel_id=1, source_target_pairs={{0,8},{4,12},{8,16},{12,20},{16,24},{20,28},{1,9},{5,13},{9,17},{1... | collective-permute-start | bytes 2752520 | tf_op jit(solution)/shard_map/ppermute | solution.py:379
  118.7 12.1 %shard_map.171 = f32[4,896,512]{2,1,0:T(8,128)S(1)} custom-call(s32[7]{0:T(128)S(1)} %stack.33.place_ref, bf16[3584,7168]{1,0:T(8,128)(2,1)} %factor_ref.17, bf16[896,512]{1,0:T(8,128)(2,1)S(1)} %copy-done.15, bf16[896,512]{1,0:T(8,128)(2,1)S(1)} %copy-done.19, bf16[896,512]{1,0:T(8,128)(2,1)S(1)} %copy-done.17, ...), custom_call_target="tpu_custom_call", output_to_operand_aliasing={{}: (14, {})} | custom-call | flops 6576668672 | bytes 12845056 | tf_op jit(solution)/shard_map/pallas_call | solution.py:90
  132.3 1.5 copy-done.4
  137.3 2.8 collective-permute-done.20.refs_6_
  142.2 1.3 stack.41.place_ref
  143.5 2.2 collective-permute-start.21
  147.1 2.2 collective-permute-start.18
  150.1 3.1 copy-done.6
  153.2 13.1 %shard_map.172.refs_8_ = f32[4,896,512]{2,1,0:T(8,128)S(1)} custom-call(s32[7]{0:T(128)S(1)} %stack.37.place_ref, bf16[3584,7168]{1,0:T(8,128)(2,1)} %factor_ref.17, bf16[896,512]{1,0:T(8,128)(2,1)S(1)} %collective-permute-done.9.refs_0_, bf16[896,512]{1,0:T(8,128)(2,1)S(1)} %collective-permute-done.23.refs_1_, ...), custom_call_target="tpu_custom_call", output_to_operand_aliasing={{}: (6, {})} | custom-call | flops 6576668672 | bytes 12845056 | tf_op jit(solution)/shard_map/pallas_call | solution.py:90
  166.3 13.2 %shard_map.173.refs_12_ = f32[4,896,512]{2,1,0:T(8,128)S(1)} custom-call(s32[7]{0:T(128)S(1)} %stack.34.place_ref, bf16[3584,7168]{1,0:T(8,128)(2,1)} %factor_ref.17, bf16[896,512]{1,0:T(8,128)(2,1)S(1)} %collective-permute-done.9.refs_0_, bf16[896,512]{1,0:T(8,128)(2,1)S(1)} %collective-permute-done.23.refs_1_, ...), custom_call_target="tpu_custom_call", output_to_operand_aliasing={{}: (10, {})} | custom-call | flops 6576668672 | bytes 12845056 | tf_op jit(solution)/shard_map/pallas_call | solution.py:90
  179.5 3.0 copy-done.7
  182.5 7.7 %collective-permute-done.16 = f16[912,512]{1,0:T(8,128)(2,1)S(1)} collective-permute-done((f16[912,512]{1,0:T(8,128)(2,1)}, f16[912,512]{1,0:T(8,128)(2,1)S(1)}, u32[]{:S(2)}, u32[]{:S(2)}) %collective-permute-start.16) | collective-permute-done | bytes 933920 | tf_op jit(solution)/shard_map/ppermute | solution.py:462
  191.0 2.6 collective-permute-start.28
  193.7 2.6 fusion.6.x_ref
  196.3 1.8 fusion.30
  198.7 7.1 %shard_map.174 = f32[2,896,512]{2,1,0:T(8,128)S(1)} custom-call(s32[5]{0:T(128)S(1)} %stack.38.place_ref, bf16[3584,7168]{1,0:T(8,128)(2,1)} %factor_ref.17, bf16[896,512]{1,0:T(8,128)(2,1)S(1)} %copy-done.11, bf16[896,512]{1,0:T(8,128)(2,1)S(1)} %copy-done.13, bf16[896,512]{1,0:T(8,128)(2,1)S(1)} %collective-permute-done.10.refs_2_, ...), custom_call_target="tpu_custom_call" | custom-call | flops 3288334336 | bytes 6422528 | tf_op jit(solution)/shard_map/pallas_call | solution.py:90
  209.6 7.1 %shard_map.175 = f32[2,896,512]{2,1,0:T(8,128)S(1)} custom-call(s32[5]{0:T(128)S(1)} %stack.41.place_ref, bf16[3584,7168]{1,0:T(8,128)(2,1)} %factor_ref.17, bf16[896,512]{1,0:T(8,128)(2,1)S(1)} %copy-done.11, bf16[896,512]{1,0:T(8,128)(2,1)S(1)} %copy-done.13, bf16[896,512]{1,0:T(8,128)(2,1)S(1)} %collective-permute-done.10.refs_2_, ...), custom_call_target="tpu_custom_call" | custom-call | flops 3288334336 | bytes 6422528 | tf_op jit(solution)/shard_map/pallas_call | solution.py:90
  217.1 1.4 copy-done.8
  218.7 2.1 collective-permute-start.32
  222.9 32.4 %collective-permute-done.33 = f32[64,512]{1,0:T(8,128)S(1)} collective-permute-done((f32[64,512]{1,0:T(8,128)S(1)}, f32[64,512]{1,0:T(8,128)S(1)}, u32[]{:S(2)}, u32[]{:S(2)}) %collective-permute-start.33) | collective-permute-done | bytes 131104 | tf_op jit(solution)/shard_map/ppermute | solution.py:502
  255.3 3.9 collective-permute-done.35
  260.8 3.2 collective-permute-start.36
  264.0 1.4 collective-permute-done.36
  268.6 1.4 convert_element_type.87
  270.1 1.6 convert_element_type.88
  271.7 1.4 convert_element_type.89
  274.1 3.5 fusion.9
  278.9 4.6 %collective-permute-start.42 = (f32[512,512]{1,0:T(8,128)S(1)}, f32[512,512]{1,0:T(8,128)}, u32[]{:S(2)}, u32[]{:S(2)}) collective-permute-start(f32[512,512]{1,0:T(8,128)S(1)} %constant_dynamic-slice_fusion.6), channel_id=1, source_target_pairs={{0,4},{4,0},{8,12},{12,8},{16,20},{20,16},{24,28},{28,24},{1,5},{5... | collective-permute-start | bytes 3145736 | tf_op jit(solution)/shard_map/ppermute | solution.py:502
  284.3 1.6 collective-permute-start.39
  289.0 2.0 collective-permute-done.40
  291.0 1.8 dynamic-slice_add_fusion
  293.6 1.8 collective-permute-start.43
  297.5 6.2 %collective-permute-done.43 = f32[64,512]{1,0:T(8,128)S(1)} collective-permute-done((f32[64,512]{1,0:T(8,128)S(1)}, f32[64,512]{1,0:T(8,128)S(1)}, u32[]{:S(2)}, u32[]{:S(2)}) %collective-permute-start.43) | collective-permute-done | bytes 131104 | tf_op jit(solution)/shard_map/ppermute | solution.py:522
  303.7 9.5 %collective-permute-done.44 = f32[64,512]{1,0:T(8,128)S(1)} collective-permute-done((f32[64,512]{1,0:T(8,128)S(1)}, f32[64,512]{1,0:T(8,128)S(1)}, u32[]{:S(2)}, u32[]{:S(2)}) %collective-permute-start.44) | collective-permute-done | bytes 131104 | tf_op jit(solution)/shard_map/ppermute | solution.py:522
  319.4 2.1 collective-permute-done.50
  321.5 2.7 collective-permute-done.51
  325.4 1.7 collective-permute-start.53
  329.5 12.4 %shard_map.176 = (f32[256,256]{1,0:T(8,128)S(1)}, f32[256,256]{1,0:T(8,128)S(1)}) custom-call(f32[256,256]{1,0:T(8,128)S(1)} %slice.128.gram_ref), custom_call_target="tpu_custom_call" | custom-call | flops 16000000000 | bytes 4000000 | tf_op jit(solution)/shard_map/pallas_call | solution.py:305
  341.9 14.5 %shard_map.177 = (f32[512,256]{1,0:T(8,128)S(1)}, f32[256,512]{1,0:T(8,128)S(1)}) custom-call(f32[512,256]{1,0:T(8,128)S(1)} %slice.129.gram_ref, f32[256,256]{1,0:T(8,128)S(1)} %get-tuple-element.120.refs_0_), custom_call_target="tpu_custom_call" | custom-call | flops 16000000000 | bytes 4000000 | tf_op jit(solution)/shard_map/pallas_call | solution.py:305
  356.7 1.6 collective-permute-start.56
  360.4 3.8 collective-permute-done.56
  364.3 7.2 %collective-permute-done.57 = f32[128,512]{1,0:T(8,128)S(1)} collective-permute-done((f32[128,512]{1,0:T(8,128)S(1)}, f32[128,512]{1,0:T(8,128)S(1)}, u32[]{:S(2)}, u32[]{:S(2)}) %collective-permute-start.57) | collective-permute-done | bytes 262176 | tf_op jit(solution)/shard_map/ppermute | solution.py:522
  372.5 1.9 shard_map.180.refs_0_
  375.0 16.2 %shard_map.178 = (f32[768,256]{1,0:T(8,128)S(1)}, f32[256,768]{1,0:T(8,128)S(1)}) custom-call(f32[768,256]{1,0:T(8,128)S(1)} %slice.130.gram_ref, f32[512,512]{1,0:T(8,128)S(1)} %select_maximum_fusion.3.refs_0_.rows_ref), custom_call_target="tpu_custom_call" | custom-call | flops 16000000000 | bytes 4000000 | tf_op jit(solution)/shard_map/pallas_call | solution.py:305
  391.4 20.4 %shard_map.179 = (f32[1024,256]{1,0:T(8,128)S(1)}, f32[256,1024]{1,0:T(8,128)S(1)}) custom-call(f32[1024,256]{1,0:T(8,128)S(1)} %slice.131.gram_ref, f32[768,768]{1,0:T(8,128)S(1)} %select_maximum_fusion.2.refs_0_), custom_call_target="tpu_custom_call" | custom-call | flops 16000000000 | bytes 4000000 | tf_op jit(solution)/shard_map/pallas_call | solution.py:305
  412.2 4.5 %shard_map.181 = f32[896,1024]{1,0:T(8,128)} custom-call(f32[896,1024]{1,0:T(8,128)S(1)} %pad_maximum_fusion.x_ref, f32[512,1024]{1,0:T(8,128)S(1)} %pad_maximum_fusion.1.rows_ref, f32[896,512]{1,0:T(8,128)S(1)} %shard_map.180.refs_0_), custom_call_target="tpu_custom_call" | custom-call | flops 2818572288 | bytes 7340032 | tf_op jit(solution)/shard_map/pallas_call | solution.py:340
  416.7 2.6 fusion
  (243 shorter events, 64.3 us)
Async XLA Ops:
  3.2 8.7 %collective-permute-start.2 = (bf16[896,512]{1,0:T(8,128)(2,1)S(1)}, bf16[896,512]{1,0:T(8,128)(2,1)}, u32[]{:S(2)}, u32[]{:S(2)}) collective-permute-start(bf16[896,512]{1,0:T(8,128)(2,1)S(1)} %get-tuple-element.152.refs_0_), channel_id=1, source_target_pairs={{0,4},{4,0},{8,12},{12,8},{16,20},{20,16},{24,28},{28,24},{1,5},{5... | collective-permute-start | bytes 2752520 | tf_op jit(solution)/shard_map/ppermute | solution.py:386
  3.2 24.6 %collective-permute-start = (bf16[896,512]{1,0:T(8,128)(2,1)S(1)}, bf16[896,512]{1,0:T(8,128)(2,1)S(1)}, u32[]{:S(2)}, u32[]{:S(2)}) collective-permute-start(bf16[896,512]{1,0:T(8,128)(2,1)S(1)} %get-tuple-element.152.refs_0_), channel_id=1, source_target_pairs={{0,8},{4,12},{8,16},{12,20},{16,24},{20,28},{1,9},{5,13},{9,17},{1... | collective-permute-start | bytes 2752520 | tf_op jit(solution)/shard_map/ppermute | solution.py:379
  7.9 23.6 %collective-permute-start.1 = (bf16[896,512]{1,0:T(8,128)(2,1)S(1)}, bf16[896,512]{1,0:T(8,128)(2,1)S(1)}, u32[]{:S(2)}, u32[]{:S(2)}) collective-permute-start(bf16[896,512]{1,0:T(8,128)(2,1)S(1)} %get-tuple-element.152.refs_0_), channel_id=1, source_target_pairs={{8,0},{12,4},{16,8},{20,12},{24,16},{28,20},{9,1},{13,5},{17,9},{2... | collective-permute-start | bytes 2752520 | tf_op jit(solution)/shard_map/ppermute | solution.py:379
  27.8 65.5 %copy-start.14 = (bf16[896,512]{1,0:T(8,128)(2,1)}, bf16[896,512]{1,0:T(8,128)(2,1)S(1)}, u32[]{:S(2)}) copy-start(bf16[896,512]{1,0:T(8,128)(2,1)S(1)} %collective-permute-done.refs_0_) | copy-start | bytes 2752516
  31.5 9.2 %collective-permute-start.5 = (bf16[896,512]{1,0:T(8,128)(2,1)S(1)}, bf16[896,512]{1,0:T(8,128)(2,1)S(1)}, u32[]{:S(2)}, u32[]{:S(2)}) collective-permute-start(bf16[896,512]{1,0:T(8,128)(2,1)S(1)} %collective-permute-done.refs_0_), channel_id=1, source_target_pairs={{0,4},{4,0},{8,12},{12,8},{16,20},{20,16},{24,28},{28,24},{1,5},{5... | collective-permute-start | bytes 2752520 | tf_op jit(solution)/shard_map/ppermute | solution.py:386
  32.6 8.1 %collective-permute-start.6 = (bf16[896,512]{1,0:T(8,128)(2,1)S(1)}, bf16[896,512]{1,0:T(8,128)(2,1)}, u32[]{:S(2)}, u32[]{:S(2)}) collective-permute-start(bf16[896,512]{1,0:T(8,128)(2,1)S(1)} %collective-permute-done.1.refs_2_), channel_id=1, source_target_pairs={{0,4},{4,0},{8,12},{12,8},{16,20},{20,16},{24,28},{28,24},{1,5},{5... | collective-permute-start | bytes 2752520 | tf_op jit(solution)/shard_map/ppermute | solution.py:386
  32.6 27.5 %collective-permute-start.3 = (bf16[896,512]{1,0:T(8,128)(2,1)S(1)}, bf16[896,512]{1,0:T(8,128)(2,1)}, u32[]{:S(2)}, u32[]{:S(2)}) collective-permute-start(bf16[896,512]{1,0:T(8,128)(2,1)S(1)} %collective-permute-done.refs_0_), channel_id=1, source_target_pairs={{0,8},{4,12},{8,16},{12,20},{16,24},{20,28},{1,9},{5,13},{9,17},{1... | collective-permute-start | bytes 2752520 | tf_op jit(solution)/shard_map/ppermute | solution.py:379
  36.7 23.5 %collective-permute-start.4 = (bf16[896,512]{1,0:T(8,128)(2,1)S(1)}, bf16[896,512]{1,0:T(8,128)(2,1)}, u32[]{:S(2)}, u32[]{:S(2)}) collective-permute-start(bf16[896,512]{1,0:T(8,128)(2,1)S(1)} %collective-permute-done.1.refs_2_), channel_id=1, source_target_pairs={{8,0},{12,4},{16,8},{20,12},{24,16},{28,20},{9,1},{13,5},{17,9},{2... | collective-permute-start | bytes 2752520 | tf_op jit(solution)/shard_map/ppermute | solution.py:379
  60.1 9.8 %collective-permute-start.13 = (bf16[896,512]{1,0:T(8,128)(2,1)}, bf16[896,512]{1,0:T(8,128)(2,1)}, u32[]{:S(2)}, u32[]{:S(2)}) collective-permute-start(bf16[896,512]{1,0:T(8,128)(2,1)} %get-tuple-element.76.refs_0_), channel_id=1, source_target_pairs={{0,4},{4,0},{8,12},{12,8},{16,20},{20,16},{24,28},{28,24},{1,5},{5... | collective-permute-start | bytes 2752520 | tf_op jit(solution)/shard_map/ppermute | solution.py:386
  61.4 9.9 %collective-permute-start.11 = (bf16[896,512]{1,0:T(8,128)(2,1)}, bf16[896,512]{1,0:T(8,128)(2,1)S(1)}, u32[]{:S(2)}, u32[]{:S(2)}) collective-permute-start(bf16[896,512]{1,0:T(8,128)(2,1)} %collective-permute-done.3.refs_4_), channel_id=1, source_target_pairs={{0,4},{4,0},{8,12},{12,8},{16,20},{20,16},{24,28},{28,24},{1,5},{5... | collective-permute-start | bytes 2752520 | tf_op jit(solution)/shard_map/ppermute | solution.py:386
  61.4 32.0 %collective-permute-start.12 = (bf16[896,512]{1,0:T(8,128)(2,1)}, bf16[896,512]{1,0:T(8,128)(2,1)}, u32[]{:S(2)}, u32[]{:S(2)}) collective-permute-start(bf16[896,512]{1,0:T(8,128)(2,1)} %collective-permute-done.4.refs_6_), channel_id=1, source_target_pairs={{0,4},{4,0},{8,12},{12,8},{16,20},{20,16},{24,28},{28,24},{1,5},{5... | collective-permute-start | bytes 2752520 | tf_op jit(solution)/shard_map/ppermute | solution.py:386
  64.5 28.9 %copy-start.17 = (bf16[896,512]{1,0:T(8,128)(2,1)S(1)}, bf16[896,512]{1,0:T(8,128)(2,1)}, u32[]{:S(2)}) copy-start(bf16[896,512]{1,0:T(8,128)(2,1)} %copy-done.16) | copy-start | bytes 2752516
  64.5 28.9 %copy-start.19 = (bf16[896,512]{1,0:T(8,128)(2,1)S(1)}, bf16[896,512]{1,0:T(8,128)(2,1)}, u32[]{:S(2)}) copy-start(bf16[896,512]{1,0:T(8,128)(2,1)} %copy-done.18) | copy-start | bytes 2752516
  64.5 42.1 %collective-permute-start.10 = (bf16[896,512]{1,0:T(8,128)(2,1)}, bf16[896,512]{1,0:T(8,128)(2,1)S(1)}, u32[]{:S(2)}, u32[]{:S(2)}) collective-permute-start(bf16[896,512]{1,0:T(8,128)(2,1)} %get-tuple-element.76.refs_0_), channel_id=1, source_target_pairs={{8,0},{12,4},{16,8},{20,12},{24,16},{28,20},{9,1},{13,5},{17,9},{2... | collective-permute-start | bytes 2752520 | tf_op jit(solution)/shard_map/ppermute | solution.py:379
  65.9 40.7 %collective-permute-start.7 = (bf16[896,512]{1,0:T(8,128)(2,1)}, bf16[896,512]{1,0:T(8,128)(2,1)S(1)}, u32[]{:S(2)}, u32[]{:S(2)}) collective-permute-start(bf16[896,512]{1,0:T(8,128)(2,1)} %collective-permute-done.3.refs_4_), channel_id=1, source_target_pairs={{0,8},{4,12},{8,16},{12,20},{16,24},{20,28},{1,9},{5,13},{9,17},{1... | collective-permute-start | bytes 2752520 | tf_op jit(solution)/shard_map/ppermute | solution.py:379
  70.0 38.4 %collective-permute-start.8 = (bf16[896,512]{1,0:T(8,128)(2,1)}, bf16[896,512]{1,0:T(8,128)(2,1)S(1)}, u32[]{:S(2)}, u32[]{:S(2)}) collective-permute-start(bf16[896,512]{1,0:T(8,128)(2,1)} %collective-permute-done.4.refs_6_), channel_id=1, source_target_pairs={{8,0},{12,4},{16,8},{20,12},{24,16},{28,20},{9,1},{13,5},{17,9},{2... | collective-permute-start | bytes 2752520 | tf_op jit(solution)/shard_map/ppermute | solution.py:379
  72.2 37.1 %collective-permute-start.9 = (bf16[896,512]{1,0:T(8,128)(2,1)}, bf16[896,512]{1,0:T(8,128)(2,1)S(1)}, u32[]{:S(2)}, u32[]{:S(2)}) collective-permute-start(bf16[896,512]{1,0:T(8,128)(2,1)} %get-tuple-element.76.refs_0_), channel_id=1, source_target_pairs={{0,8},{4,12},{8,16},{12,20},{16,24},{20,28},{1,9},{5,13},{9,17},{1... | collective-permute-start | bytes 2752520 | tf_op jit(solution)/shard_map/ppermute | solution.py:379
  109.3 56.9 %copy-start.10 = (bf16[896,512]{1,0:T(8,128)(2,1)}, bf16[896,512]{1,0:T(8,128)(2,1)S(1)}, u32[]{:S(2)}) copy-start(bf16[896,512]{1,0:T(8,128)(2,1)S(1)} %collective-permute-done.9.refs_0_) | copy-start | bytes 2752516
  109.3 8.1 %collective-permute-start.14 = (bf16[896,512]{1,0:T(8,128)(2,1)S(1)}, bf16[896,512]{1,0:T(8,128)(2,1)S(1)}, u32[]{:S(2)}, u32[]{:S(2)}) collective-permute-start(bf16[896,512]{1,0:T(8,128)(2,1)S(1)} %collective-permute-done.7.refs_8_), channel_id=1, source_target_pairs={{0,4},{4,0},{8,12},{12,8},{16,20},{20,16},{24,28},{28,24},{1,5},{5... | collective-permute-start | bytes 2752520 | tf_op jit(solution)/shard_map/ppermute | solution.py:386
  110.4 7.1 %collective-permute-start.15 = (bf16[896,512]{1,0:T(8,128)(2,1)S(1)}, bf16[896,512]{1,0:T(8,128)(2,1)S(1)}, u32[]{:S(2)}, u32[]{:S(2)}) collective-permute-start(bf16[896,512]{1,0:T(8,128)(2,1)S(1)} %collective-permute-done.8.refs_10_), channel_id=1, source_target_pairs={{0,4},{4,0},{8,12},{12,8},{16,20},{20,16},{24,28},{28,24},{1,5},{5... | collective-permute-start | bytes 2752520 | tf_op jit(solution)/shard_map/ppermute | solution.py:386
  110.4 26.9 %collective-permute-start.19 = (bf16[896,512]{1,0:T(8,128)(2,1)S(1)}, bf16[896,512]{1,0:T(8,128)(2,1)}, u32[]{:S(2)}, u32[]{:S(2)}) collective-permute-start(bf16[896,512]{1,0:T(8,128)(2,1)S(1)} %collective-permute-done.9.refs_0_), channel_id=1, source_target_pairs={{0,8},{4,12},{8,16},{12,20},{16,24},{20,28},{1,9},{5,13},{9,17},{1... | collective-permute-start | bytes 2752520 | tf_op jit(solution)/shard_map/ppermute | solution.py:379
  115.4 30.4 %collective-permute-start.23 = (bf16[896,512]{1,0:T(8,128)(2,1)S(1)}, bf16[896,512]{1,0:T(8,128)(2,1)S(1)}, u32[]{:S(2)}, u32[]{:S(2)}) collective-permute-start(bf16[896,512]{1,0:T(8,128)(2,1)S(1)} %collective-permute-done.9.refs_0_), channel_id=1, source_target_pairs={{0,4},{4,0},{8,12},{12,8},{16,20},{20,16},{24,28},{28,24},{1,5},{5... | collective-permute-start | bytes 2752520 | tf_op jit(solution)/shard_map/ppermute | solution.py:386
  116.2 24.0 %collective-permute-start.20 = (bf16[896,512]{1,0:T(8,128)(2,1)S(1)}, bf16[896,512]{1,0:T(8,128)(2,1)}, u32[]{:S(2)}, u32[]{:S(2)}) collective-permute-start(bf16[896,512]{1,0:T(8,128)(2,1)S(1)} %collective-permute-done.10.refs_2_), channel_id=1, source_target_pairs={{8,0},{12,4},{16,8},{20,12},{24,16},{28,20},{9,1},{13,5},{17,9},{2... | collective-permute-start | bytes 2752520 | tf_op jit(solution)/shard_map/ppermute | solution.py:379
  117.4 29.7 %collective-permute-start.24 = (bf16[896,512]{1,0:T(8,128)(2,1)S(1)}, bf16[896,512]{1,0:T(8,128)(2,1)}, u32[]{:S(2)}, u32[]{:S(2)}) collective-permute-start(bf16[896,512]{1,0:T(8,128)(2,1)S(1)} %collective-permute-done.10.refs_2_), channel_id=1, source_target_pairs={{0,4},{4,0},{8,12},{12,8},{16,20},{20,16},{24,28},{28,24},{1,5},{5... | collective-permute-start | bytes 2752520 | tf_op jit(solution)/shard_map/ppermute | solution.py:386
  140.1 9.2 %collective-permute-start.25 = (bf16[896,512]{1,0:T(8,128)(2,1)}, bf16[896,512]{1,0:T(8,128)(2,1)}, u32[]{:S(2)}, u32[]{:S(2)}) collective-permute-start(bf16[896,512]{1,0:T(8,128)(2,1)} %collective-permute-done.19.refs_4_), channel_id=1, source_target_pairs={{0,4},{4,0},{8,12},{12,8},{16,20},{20,16},{24,28},{28,24},{1,5},{5... | collective-permute-start | bytes 2752520 | tf_op jit(solution)/shard_map/ppermute | solution.py:386
  140.9 8.7 %collective-permute-start.26 = (bf16[896,512]{1,0:T(8,128)(2,1)}, bf16[896,512]{1,0:T(8,128)(2,1)}, u32[]{:S(2)}, u32[]{:S(2)}) collective-permute-start(bf16[896,512]{1,0:T(8,128)(2,1)} %collective-permute-done.20.refs_6_), channel_id=1, source_target_pairs={{0,4},{4,0},{8,12},{12,8},{16,20},{20,16},{24,28},{28,24},{1,5},{5... | collective-permute-start | bytes 2752520 | tf_op jit(solution)/shard_map/ppermute | solution.py:386
  143.5 38.9 %collective-permute-start.21 = (bf16[896,512]{1,0:T(8,128)(2,1)}, bf16[896,512]{1,0:T(8,128)(2,1)S(1)}, u32[]{:S(2)}, u32[]{:S(2)}) collective-permute-start(bf16[896,512]{1,0:T(8,128)(2,1)} %collective-permute-done.19.refs_4_), channel_id=1, source_target_pairs={{0,8},{4,12},{8,16},{12,20},{16,24},{20,28},{1,9},{5,13},{9,17},{1... | collective-permute-start | bytes 2752520 | tf_op jit(solution)/shard_map/ppermute | solution.py:379
  145.8 36.6 %collective-permute-start.22 = (bf16[896,512]{1,0:T(8,128)(2,1)}, bf16[896,512]{1,0:T(8,128)(2,1)S(1)}, u32[]{:S(2)}, u32[]{:S(2)}) collective-permute-start(bf16[896,512]{1,0:T(8,128)(2,1)} %collective-permute-done.20.refs_6_), channel_id=1, source_target_pairs={{8,0},{12,4},{16,8},{20,12},{24,16},{28,20},{9,1},{13,5},{17,9},{2... | collective-permute-start | bytes 2752520 | tf_op jit(solution)/shard_map/ppermute | solution.py:379
  147.1 35.3 %collective-permute-start.18 = (f16[912,512]{1,0:T(8,128)(2,1)}, f16[912,512]{1,0:T(8,128)(2,1)S(1)}, u32[]{:S(2)}, u32[]{:S(2)}) collective-permute-start(f16[912,512]{1,0:T(8,128)(2,1)} %pad_maximum_fusion.4), channel_id=1, source_target_pairs={{0,3},{1,0},{2,1},{3,2},{4,7},{5,4},{6,5},{7,6},{8,11},{9,8},{10,9... | collective-permute-start | bytes 2801672 | tf_op jit(solution)/shard_map/ppermute | solution.py:462
  149.4 33.1 %collective-permute-start.17 = (f16[912,512]{1,0:T(8,128)(2,1)}, f16[912,512]{1,0:T(8,128)(2,1)S(1)}, u32[]{:S(2)}, u32[]{:S(2)}) collective-permute-start(f16[912,512]{1,0:T(8,128)(2,1)} %pad_maximum_fusion.3), channel_id=1, source_target_pairs={{0,2},{1,3},{2,0},{3,1},{4,6},{5,7},{6,4},{7,5},{8,10},{9,11},{10,... | collective-permute-start | bytes 2801672 | tf_op jit(solution)/shard_map/ppermute | solution.py:462
  149.6 40.6 %collective-permute-start.16 = (f16[912,512]{1,0:T(8,128)(2,1)}, f16[912,512]{1,0:T(8,128)(2,1)S(1)}, u32[]{:S(2)}, u32[]{:S(2)}) collective-permute-start(f16[912,512]{1,0:T(8,128)(2,1)} %pad_maximum_fusion.2), channel_id=1, source_target_pairs={{0,1},{1,2},{2,3},{3,0},{4,5},{5,6},{6,7},{7,4},{8,9},{9,10},{10,1... | collective-permute-start | bytes 2801672 | tf_op jit(solution)/shard_map/ppermute | solution.py:462
  191.0 7.7 %collective-permute-start.28 = (bf16[896,512]{1,0:T(8,128)(2,1)S(1)}, bf16[896,512]{1,0:T(8,128)(2,1)S(1)}, u32[]{:S(2)}, u32[]{:S(2)}) collective-permute-start(bf16[896,512]{1,0:T(8,128)(2,1)S(1)} %collective-permute-done.21.refs_8_), channel_id=1, source_target_pairs={{0,4},{4,0},{8,12},{12,8},{16,20},{20,16},{24,28},{28,24},{1,5},{5... | collective-permute-start | bytes 2752520 | tf_op jit(solution)/shard_map/ppermute | solution.py:386
  193.6 5.1 %collective-permute-start.29 = (bf16[896,512]{1,0:T(8,128)(2,1)S(1)}, bf16[896,512]{1,0:T(8,128)(2,1)S(1)}, u32[]{:S(2)}, u32[]{:S(2)}) collective-permute-start(bf16[896,512]{1,0:T(8,128)(2,1)S(1)} %collective-permute-done.22.refs_10_), channel_id=1, source_target_pairs={{0,4},{4,0},{8,12},{12,8},{16,20},{20,16},{24,28},{28,24},{1,5},{5... | collective-permute-start | bytes 2752520 | tf_op jit(solution)/shard_map/ppermute | solution.py:386
  198.2 11.4 %collective-permute-start.27 = (f32[256,512]{1,0:T(8,128)S(1)}, f32[256,512]{1,0:T(8,128)S(1)}, u32[]{:S(2)}, u32[]{:S(2)}) collective-permute-start(f32[256,512]{1,0:T(8,128)S(1)} %constant_dynamic-slice_fusion.13), channel_id=1, source_target_pairs={{0,4},{4,0},{8,12},{12,8},{16,20},{20,16},{24,28},{28,24},{1,5},{5... | collective-permute-start | bytes 1572872 | tf_op jit(solution)/shard_map/ppermute | solution.py:502
  207.8 60.8 %collective-permute-start.31 = (f16[912,512]{1,0:T(8,128)(2,1)}, f16[912,512]{1,0:T(8,128)(2,1)}, u32[]{:S(2)}, u32[]{:S(2)}) collective-permute-start(f16[912,512]{1,0:T(8,128)(2,1)} %pad_maximum_fusion.6), channel_id=1, source_target_pairs={{0,2},{1,3},{2,0},{3,1},{4,6},{5,7},{6,4},{7,5},{8,10},{9,11},{10,... | collective-permute-start | bytes 2801672 | tf_op jit(solution)/shard_map/ppermute | solution.py:462
  209.3 59.4 %collective-permute-start.30 = (f16[912,512]{1,0:T(8,128)(2,1)}, f16[912,512]{1,0:T(8,128)(2,1)}, u32[]{:S(2)}, u32[]{:S(2)}) collective-permute-start(f16[912,512]{1,0:T(8,128)(2,1)} %pad_maximum_fusion.5), channel_id=1, source_target_pairs={{0,1},{1,2},{2,3},{3,0},{4,5},{5,6},{6,7},{7,4},{8,9},{9,10},{10,1... | collective-permute-start | bytes 2801672 | tf_op jit(solution)/shard_map/ppermute | solution.py:462
  218.7 49.9 %collective-permute-start.32 = (f16[912,512]{1,0:T(8,128)(2,1)S(1)}, f16[912,512]{1,0:T(8,128)(2,1)}, u32[]{:S(2)}, u32[]{:S(2)}) collective-permute-start(f16[912,512]{1,0:T(8,128)(2,1)S(1)} %pad_maximum_fusion.7), channel_id=1, source_target_pairs={{0,3},{1,0},{2,1},{3,2},{4,7},{5,4},{6,5},{7,6},{8,11},{9,8},{10,9... | collective-permute-start | bytes 2801672 | tf_op jit(solution)/shard_map/ppermute | solution.py:462
  221.6 33.6 %collective-permute-start.33 = (f32[64,512]{1,0:T(8,128)S(1)}, f32[64,512]{1,0:T(8,128)S(1)}, u32[]{:S(2)}, u32[]{:S(2)}) collective-permute-start(f32[64,512]{1,0:T(8,128)S(1)} %get-tuple-element.159), channel_id=1, source_target_pairs={{0,1},{1,2},{2,3},{3,0},{4,5},{5,6},{6,7},{7,4},{8,9},{9,10},{10,1... | collective-permute-start | bytes 393224 | tf_op jit(solution)/shard_map/ppermute | solution.py:502
  221.7 33.6 %collective-permute-start.34 = (f32[64,512]{1,0:T(8,128)}, f32[64,512]{1,0:T(8,128)}, u32[]{:S(2)}, u32[]{:S(2)}) collective-permute-start(f32[64,512]{1,0:T(8,128)} %get-tuple-element.158), channel_id=1, source_target_pairs={{0,2},{1,3},{2,0},{3,1},{4,6},{5,7},{6,4},{7,5},{8,10},{9,11},{10,... | collective-permute-start | bytes 393224 | tf_op jit(solution)/shard_map/ppermute | solution.py:502
  255.2 3.9 collective-permute-start.35
  260.8 4.6 %collective-permute-start.36 = (f32[16,512]{1,0:T(8,128)S(1)}, f32[16,512]{1,0:T(8,128)S(1)}, u32[]{:S(2)}, u32[]{:S(2)}) collective-permute-start(f32[16,512]{1,0:T(8,128)S(1)} %get-tuple-element.165), channel_id=1, source_target_pairs={{0,8},{4,12},{8,16},{12,20},{16,24},{20,28},{24,0},{28,4},{1,9},{5... | collective-permute-start | bytes 98312 | tf_op jit(solution)/shard_map/ppermute | solution.py:502
  264.0 3.8 collective-permute-start.37
  265.4 3.2 collective-permute-start.38
  278.9 12.1 %collective-permute-start.42 = (f32[512,512]{1,0:T(8,128)S(1)}, f32[512,512]{1,0:T(8,128)}, u32[]{:S(2)}, u32[]{:S(2)}) collective-permute-start(f32[512,512]{1,0:T(8,128)S(1)} %constant_dynamic-slice_fusion.6), channel_id=1, source_target_pairs={{0,4},{4,0},{8,12},{12,8},{16,20},{20,16},{24,28},{28,24},{1,5},{5... | collective-permute-start | bytes 3145736 | tf_op jit(solution)/shard_map/ppermute | solution.py:502
  284.3 4.6 %collective-permute-start.39 = (f32[16,512]{1,0:T(8,128)S(1)}, f32[16,512]{1,0:T(8,128)S(1)}, u32[]{:S(2)}, u32[]{:S(2)}) collective-permute-start(f32[16,512]{1,0:T(8,128)S(1)} %get-tuple-element.146), channel_id=1, source_target_pairs={{0,8},{4,12},{8,16},{12,20},{16,24},{20,28},{24,0},{28,4},{1,9},{5... | collective-permute-start | bytes 98312 | tf_op jit(solution)/shard_map/ppermute | solution.py:522
  285.9 5.1 %collective-permute-start.40 = (f32[16,512]{1,0:T(8,128)S(1)}, f32[16,512]{1,0:T(8,128)S(1)}, u32[]{:S(2)}, u32[]{:S(2)}) collective-permute-start(f32[16,512]{1,0:T(8,128)S(1)} %get-tuple-element.146), channel_id=1, source_target_pairs={{0,16},{4,20},{8,24},{12,28},{16,0},{20,4},{24,8},{28,12},{1,17},{... | collective-permute-start | bytes 98312 | tf_op jit(solution)/shard_map/ppermute | solution.py:522
  287.1 3.9 collective-permute-start.41
  292.8 20.4 %collective-permute-start.46 = (f32[128,512]{1,0:T(8,128)S(1)}, f32[128,512]{1,0:T(8,128)S(1)}, u32[]{:S(2)}, u32[]{:S(2)}) collective-permute-start(f32[128,512]{1,0:T(8,128)S(1)} %get-tuple-element.156), channel_id=1, source_target_pairs={{0,1},{1,2},{2,3},{3,0},{4,5},{5,6},{6,7},{7,4},{8,9},{9,10},{10,1... | collective-permute-start | bytes 786440 | tf_op jit(solution)/shard_map/ppermute | solution.py:502
  293.6 10.1 %collective-permute-start.43 = (f32[64,512]{1,0:T(8,128)S(1)}, f32[64,512]{1,0:T(8,128)S(1)}, u32[]{:S(2)}, u32[]{:S(2)}) collective-permute-start(f32[64,512]{1,0:T(8,128)S(1)} %constant_dynamic-update-slice_fusion.16), channel_id=1, source_target_pairs={{0,1},{1,2},{2,3},{3,0},{4,5},{5,6},{6,7},{7,4},{8,9},{9,10},{10,1... | collective-permute-start | bytes 393224 | tf_op jit(solution)/shard_map/ppermute | solution.py:522
  295.3 17.9 %collective-permute-start.47 = (f32[128,512]{1,0:T(8,128)S(1)}, f32[128,512]{1,0:T(8,128)S(1)}, u32[]{:S(2)}, u32[]{:S(2)}) collective-permute-start(f32[128,512]{1,0:T(8,128)S(1)} %get-tuple-element.155), channel_id=1, source_target_pairs={{0,2},{1,3},{2,0},{3,1},{4,6},{5,7},{6,4},{7,5},{8,10},{9,11},{10,... | collective-permute-start | bytes 786440 | tf_op jit(solution)/shard_map/ppermute | solution.py:502
  295.6 17.7 %collective-permute-start.48 = (f32[128,512]{1,0:T(8,128)S(1)}, f32[128,512]{1,0:T(8,128)S(1)}, u32[]{:S(2)}, u32[]{:S(2)}) collective-permute-start(f32[128,512]{1,0:T(8,128)S(1)} %get-tuple-element.154), channel_id=1, source_target_pairs={{0,3},{1,0},{2,1},{3,2},{4,7},{5,4},{6,5},{7,6},{8,11},{9,8},{10,9... | collective-permute-start | bytes 786440 | tf_op jit(solution)/shard_map/ppermute | solution.py:502
  296.6 16.6 %collective-permute-start.44 = (f32[64,512]{1,0:T(8,128)S(1)}, f32[64,512]{1,0:T(8,128)S(1)}, u32[]{:S(2)}, u32[]{:S(2)}) collective-permute-start(f32[64,512]{1,0:T(8,128)S(1)} %constant_dynamic-update-slice_fusion.16), channel_id=1, source_target_pairs={{0,2},{1,3},{2,0},{3,1},{4,6},{5,7},{6,4},{7,5},{8,10},{9,11},{10,... | collective-permute-start | bytes 393224 | tf_op jit(solution)/shard_map/ppermute | solution.py:522
  303.6 9.6 %collective-permute-start.45 = (f32[64,512]{1,0:T(8,128)S(1)}, f32[64,512]{1,0:T(8,128)S(1)}, u32[]{:S(2)}, u32[]{:S(2)}) collective-permute-start(f32[64,512]{1,0:T(8,128)S(1)} %constant_dynamic-update-slice_fusion.16), channel_id=1, source_target_pairs={{0,3},{1,0},{2,1},{3,2},{4,7},{5,4},{6,5},{7,6},{8,11},{9,8},{10,9... | collective-permute-start | bytes 393224 | tf_op jit(solution)/shard_map/ppermute | solution.py:522
  314.1 10.1 %collective-permute-start.49 = (f32[256,512]{1,0:T(8,128)S(1)}, f32[256,512]{1,0:T(8,128)}, u32[]{:S(2)}, u32[]{:S(2)}) collective-permute-start(f32[256,512]{1,0:T(8,128)S(1)} %constant_dynamic-update-slice_fusion.12), channel_id=1, source_target_pairs={{0,4},{4,0},{8,12},{12,8},{16,20},{20,16},{24,28},{28,24},{1,5},{5... | collective-permute-start | bytes 1572872 | tf_op jit(solution)/shard_map/ppermute | solution.py:522
  315.9 5.6 %collective-permute-start.50 = (f32[32,512]{1,0:T(8,128)S(1)}, f32[32,512]{1,0:T(8,128)S(1)}, u32[]{:S(2)}, u32[]{:S(2)}) collective-permute-start(f32[32,512]{1,0:T(8,128)S(1)} %get-tuple-element.162), channel_id=1, source_target_pairs={{0,8},{4,12},{8,16},{12,20},{16,24},{20,28},{24,0},{28,4},{1,9},{5... | collective-permute-start | bytes 196616 | tf_op jit(solution)/shard_map/ppermute | solution.py:502
  316.7 7.5 %collective-permute-start.51 = (f32[32,512]{1,0:T(8,128)S(1)}, f32[32,512]{1,0:T(8,128)S(1)}, u32[]{:S(2)}, u32[]{:S(2)}) collective-permute-start(f32[32,512]{1,0:T(8,128)S(1)} %get-tuple-element.161), channel_id=1, source_target_pairs={{0,16},{4,20},{8,24},{12,28},{16,0},{20,4},{24,8},{28,12},{1,17},{... | collective-permute-start | bytes 196616 | tf_op jit(solution)/shard_map/ppermute | solution.py:502
  317.9 6.3 %collective-permute-start.52 = (f32[32,512]{1,0:T(8,128)S(1)}, f32[32,512]{1,0:T(8,128)S(1)}, u32[]{:S(2)}, u32[]{:S(2)}) collective-permute-start(f32[32,512]{1,0:T(8,128)S(1)} %get-tuple-element.160), channel_id=1, source_target_pairs={{0,24},{4,28},{8,0},{12,4},{16,8},{20,12},{24,16},{28,20},{1,25},{... | collective-permute-start | bytes 196616 | tf_op jit(solution)/shard_map/ppermute | solution.py:502
  325.4 31.2 %collective-permute-start.53 = (f32[32,512]{1,0:T(8,128)S(1)}, f32[32,512]{1,0:T(8,128)S(1)}, u32[]{:S(2)}, u32[]{:S(2)}) collective-permute-start(f32[32,512]{1,0:T(8,128)S(1)} %get-tuple-element.144), channel_id=1, source_target_pairs={{0,8},{4,12},{8,16},{12,20},{16,24},{20,28},{24,0},{28,4},{1,9},{5... | collective-permute-start | bytes 196616 | tf_op jit(solution)/shard_map/ppermute | solution.py:522
  327.1 29.5 %collective-permute-start.54 = (f32[32,512]{1,0:T(8,128)S(1)}, f32[32,512]{1,0:T(8,128)S(1)}, u32[]{:S(2)}, u32[]{:S(2)}) collective-permute-start(f32[32,512]{1,0:T(8,128)S(1)} %get-tuple-element.144), channel_id=1, source_target_pairs={{0,16},{4,20},{8,24},{12,28},{16,0},{20,4},{24,8},{28,12},{1,17},{... | collective-permute-start | bytes 196616 | tf_op jit(solution)/shard_map/ppermute | solution.py:522
  328.3 28.4 %collective-permute-start.55 = (f32[32,512]{1,0:T(8,128)S(1)}, f32[32,512]{1,0:T(8,128)S(1)}, u32[]{:S(2)}, u32[]{:S(2)}) collective-permute-start(f32[32,512]{1,0:T(8,128)S(1)} %get-tuple-element.144), channel_id=1, source_target_pairs={{0,24},{4,28},{8,0},{12,4},{16,8},{20,12},{24,16},{28,20},{1,25},{... | collective-permute-start | bytes 196616 | tf_op jit(solution)/shard_map/ppermute | solution.py:522
  356.7 7.6 %collective-permute-start.56 = (f32[128,512]{1,0:T(8,128)S(1)}, f32[128,512]{1,0:T(8,128)S(1)}, u32[]{:S(2)}, u32[]{:S(2)}) collective-permute-start(f32[128,512]{1,0:T(8,128)S(1)} %constant_dynamic-update-slice_fusion.6), channel_id=1, source_target_pairs={{0,1},{1,2},{2,3},{3,0},{4,5},{5,6},{6,7},{7,4},{8,9},{9,10},{10,1... | collective-permute-start | bytes 786440 | tf_op jit(solution)/shard_map/ppermute | solution.py:522
  358.3 13.2 %collective-permute-start.57 = (f32[128,512]{1,0:T(8,128)S(1)}, f32[128,512]{1,0:T(8,128)S(1)}, u32[]{:S(2)}, u32[]{:S(2)}) collective-permute-start(f32[128,512]{1,0:T(8,128)S(1)} %constant_dynamic-update-slice_fusion.6), channel_id=1, source_target_pairs={{0,2},{1,3},{2,0},{3,1},{4,6},{5,7},{6,4},{7,5},{8,10},{9,11},{10,... | collective-permute-start | bytes 786440 | tf_op jit(solution)/shard_map/ppermute | solution.py:522
  359.2 12.3 %collective-permute-start.58 = (f32[128,512]{1,0:T(8,128)S(1)}, f32[128,512]{1,0:T(8,128)S(1)}, u32[]{:S(2)}, u32[]{:S(2)}) collective-permute-start(f32[128,512]{1,0:T(8,128)S(1)} %constant_dynamic-update-slice_fusion.6), channel_id=1, source_target_pairs={{0,3},{1,0},{2,1},{3,2},{4,7},{5,4},{6,5},{7,6},{8,11},{9,8},{10,9... | collective-permute-start | bytes 786440 | tf_op jit(solution)/shard_map/ppermute | solution.py:522
  371.6 3.2 collective-permute-start.59
  (33 other events, 280.2 us)
